TPU v7x, 32 devices: a whole 2x2x4 slice. The times are simulated.
32 devices in a mesh: dp: 8 (over y, x, core), blk: 4 (over z).
Axes of the slice: x: 2, y: 2, z: 4, core: 2. Of those that a mesh axis runs over, the one named last changes fastest.
Arguments:
- patches: bfloat16 [8, 576, 768], P('dp', 'blk'), may hold values from -6 to 6
- keep: int32 [8, 576], P('dp', 'blk'), may hold values from 0 to 1, as said below
- coords: int32 [2, 8, 576], P(None, 'dp', 'blk'), may hold values from 0 to 23, as said below
- query_w: bfloat16 [2, 768, 768], replicated, may hold values from -0.21875 to 0.21875
- key_w: bfloat16 [2, 768, 768], replicated, may hold values from -0.21875 to 0.21875
- value_w: bfloat16 [2, 768, 768], replicated, may hold values from -0.21875 to 0.21875
- proj_w: bfloat16 [2, 768, 768], replicated, may hold values from -0.875 to 0.875
- up_w: bfloat16 [2, 768, 3072], replicated, may hold values from -0.21875 to 0.21875
- down_w: bfloat16 [2, 3072, 768], replicated, may hold values from -0.109375 to 0.109375
- norm1_gain: float32 [2, 768], replicated, may hold values from 0.25 to 1.75
- norm1_bias: float32 [2, 768], replicated, may hold values from -3 to 3
- norm2_gain: float32 [2, 768], replicated, may hold values from 0.25 to 1.75
- norm2_bias: float32 [2, 768], replicated, may hold values from -3 to 3
- freqs: float32 [2, 2, 12, 32], replicated, may hold values from -2.5 to 2.5
- cotangent: bfloat16 [8, 576, 768], P('dp', 'blk'), may hold values from -6 to 6
Outputs:
- output: bfloat16 [8, 576, 768], P('dp', 'blk')
- grad_patches: float32 [8, 576, 768], P('dp', 'blk')
- grad_query: float32 [2, 768, 768], P(None, 'dp', 'blk')
- grad_key: float32 [2, 768, 768], P(None, 'dp', 'blk')
- grad_value: float32 [2, 768, 768], P(None, 'dp', 'blk')
- grad_proj: float32 [2, 768, 768], P(None, 'dp', 'blk')
- grad_up: float32 [2, 768, 3072], P(None, 'dp', 'blk')
- grad_down: float32 [2, 3072, 768], P(None, 'dp', 'blk')
- grad_norm1_gain: float32 [2, 768], P(None, 'blk')
- grad_norm1_bias: float32 [2, 768], P(None, 'blk')
- grad_norm2_gain: float32 [2, 768], P(None, 'blk')
- grad_norm2_bias: float32 [2, 768], P(None, 'blk')
- grad_freqs: float32 [2, 2, 12, 32], P(None, None, 'blk')
Inputs may be any that keep to these rules, and one draw needn't show every extreme that they name: `keep`: each image keeps at least one patch in every aligned run of 144 of its patches. For each image, the pairs (coords[0], coords[1]) run over the 576 cells of a 24 x 24 grid, each once.
All inputs are finite; a program needn't handle non-finite values.
Results may differ from a plain program's by a relative error of at most 0.028.
Values may be sent and summed in bfloat16 or wider, within the bound.
A program may use at most 576 MiB of HBM per device.

v0:
```python
import jax
import jax.numpy as jnp
from jax import lax
from jax.sharding import PartitionSpec as P

MASKED_SCORE = -1e30
NORM_EPSILON = 1e-06
PRECISE = lax.Precision.HIGHEST


def passed_along(block, axis, distance):
    devices = range(lax.axis_size(axis))
    route = [((i - distance) % len(devices), i) for i in devices]
    return lax.ppermute(block, axis, route)


def layer_norm(values, weight_gain, weight_bias):
    centre = values - jnp.mean(values, axis=-1, keepdims=True)
    spread = jnp.mean(centre * centre, axis=-1, keepdims=True)
    return centre * lax.rsqrt(spread + NORM_EPSILON) * weight_gain + weight_bias


def exact_gelu(values):
    return jax.nn.gelu(values, approximate=False)


def rotate(tensor, cosine, sine_part):
    halfway = tensor.shape[-1] // 2
    former = tensor[..., :halfway]
    latter = tensor[..., halfway:]
    return jnp.concatenate(
        [former * cosine - latter * sine_part, former * sine_part + latter * cosine], axis=-1
    )


def unrotate(tensor, cosine, sine_part):
    halfway = tensor.shape[-1] // 2
    former = tensor[..., :halfway]
    latter = tensor[..., halfway:]
    return jnp.concatenate(
        [former * cosine + latter * sine_part, latter * cosine - former * sine_part], axis=-1
    )


def angle_grad(grad_rotated, rotated):
    halfway = rotated.shape[-1] // 2
    return (
        grad_rotated[..., halfway:] * rotated[..., :halfway]
        - grad_rotated[..., :halfway] * rotated[..., halfway:]
    )


def times_transposed(left_side, weight):
    return lax.dot_general(
        left_side, weight, (((1,), (1,)), ((), ())), preferred_element_type=jnp.float32
    )


def outer_sum(left_side, right_side):
    return lax.dot_general(
        left_side, right_side, (((0,), (0,)), ((), ())), preferred_element_type=jnp.float32
    )


def scores_of(queries, key_rows, kept_rows):
    scaled = 0.125 * jnp.einsum(
        "iqhd,ikhd->ihqk", queries, key_rows, preferred_element_type=jnp.float32
    )
    return jnp.where(kept_rows[:, None, None, :] > 0, scaled, MASKED_SCORE)


def merge_block(running, queries, key_rows, value_rows, kept_rows):
    highest, denominator, weighted = running
    masked = scores_of(queries, key_rows, kept_rows)
    new_highest = jnp.maximum(highest, jnp.max(masked, axis=-1))
    exponent = jnp.where(
        kept_rows[:, None, None, :] > 0, jnp.exp(masked - new_highest[..., None]), 0.0
    )
    factor = jnp.exp(highest - new_highest)
    denominator = factor * denominator + jnp.sum(exponent, axis=-1)
    weighted = factor[..., None] * weighted + jnp.einsum(
        "ihqk,ikhd->ihqd", exponent, value_rows.astype(jnp.float32), precision=PRECISE
    )
    return (new_highest, denominator, weighted)


def block_grads(queries, grad_attended, log_total, delta_rows, key_rows, value_rows, kept_rows):
    masked = scores_of(queries, key_rows, kept_rows)
    weights = jnp.where(
        kept_rows[:, None, None, :] > 0, jnp.exp(masked - log_total[..., None]), 0.0
    )
    grad_weights = jnp.einsum(
        "iqhd,ikhd->ihqk", grad_attended, value_rows, preferred_element_type=jnp.float32
    )
    grad_scores = (weights * (grad_weights - delta_rows[..., None])).astype(jnp.bfloat16)
    query_part = 0.125 * jnp.einsum(
        "ihqk,ikhd->iqhd", grad_scores, key_rows, preferred_element_type=jnp.float32
    )
    key_part = 0.125 * jnp.einsum(
        "ihqk,iqhd->ikhd", grad_scores, queries, preferred_element_type=jnp.float32
    )
    value_part = jnp.einsum(
        "ihqk,iqhd->ikhd", weights, grad_attended.astype(jnp.float32), precision=PRECISE
    )
    return (query_part, key_part, value_part)


def reduce_layer(grads):
    shares = (
        lax.psum_scatter(
            grads[0].astype(jnp.bfloat16), "blk", scatter_dimension=1, tiled=True
        ).astype(jnp.float32),
        lax.psum_scatter(
            grads[1].astype(jnp.bfloat16), "blk", scatter_dimension=1, tiled=True
        ).astype(jnp.float32),
        lax.psum_scatter(
            grads[2].astype(jnp.bfloat16), "blk", scatter_dimension=1, tiled=True
        ).astype(jnp.float32),
        lax.psum_scatter(
            grads[3].astype(jnp.bfloat16), "blk", scatter_dimension=1, tiled=True
        ).astype(jnp.float32),
        lax.psum_scatter(
            grads[4].astype(jnp.bfloat16), "blk", scatter_dimension=1, tiled=True
        ).astype(jnp.float32),
        lax.psum_scatter(
            grads[5].astype(jnp.bfloat16), "blk", scatter_dimension=1, tiled=True
        ).astype(jnp.float32),
        lax.psum_scatter(
            grads[6].astype(jnp.bfloat16), "blk", scatter_dimension=0, tiled=True
        ).astype(jnp.float32),
        lax.psum_scatter(
            grads[7].astype(jnp.bfloat16), "blk", scatter_dimension=0, tiled=True
        ).astype(jnp.float32),
        lax.psum_scatter(
            grads[8].astype(jnp.bfloat16), "blk", scatter_dimension=0, tiled=True
        ).astype(jnp.float32),
        lax.psum_scatter(
            grads[9].astype(jnp.bfloat16), "blk", scatter_dimension=0, tiled=True
        ).astype(jnp.float32),
        lax.psum_scatter(
            grads[10].astype(jnp.bfloat16), "blk", scatter_dimension=1, tiled=True
        ).astype(jnp.float32),
    )
    large_part = (
        lax.psum_scatter(shares[0], "dp", scatter_dimension=0, tiled=True),
        lax.psum_scatter(shares[1], "dp", scatter_dimension=0, tiled=True),
        lax.psum_scatter(shares[2], "dp", scatter_dimension=0, tiled=True),
        lax.psum_scatter(shares[3], "dp", scatter_dimension=0, tiled=True),
        lax.psum_scatter(shares[4], "dp", scatter_dimension=0, tiled=True),
        lax.psum_scatter(shares[5], "dp", scatter_dimension=0, tiled=True),
    )
    small_part = lax.psum((shares[6], shares[7], shares[8], shares[9], shares[10]), "dp")
    return tuple(large_part) + tuple(small_part)


def shards(
    patches,
    keep,
    coords,
    query_w,
    key_w,
    value_w,
    proj_w,
    up_w,
    down_w,
    norm1_gain,
    norm1_bias,
    norm2_gain,
    norm2_bias,
    freqs,
    cotangent,
):
    images, patch_rows, model_width = patches.shape
    head_count = freqs.shape[2]
    head_dim = model_width // head_count
    token_rows = images * patch_rows
    layer_count = query_w.shape[0]
    cycle_size = lax.axis_size("blk")
    shape_four = (images, patch_rows, head_count, head_dim)
    kept_low = keep.astype(jnp.bfloat16)
    row_coord = coords[0].astype(jnp.float32)[:, :, None, None]
    column_coord = coords[1].astype(jnp.float32)[:, :, None, None]
    residual = patches.astype(jnp.float32).reshape(token_rows, model_width)
    stored = []
    for layer_no in range(layer_count):
        normed, norm_back = jax.vjp(
            layer_norm, residual, norm1_gain[layer_no], norm1_bias[layer_no]
        )
        normed_low = normed.astype(jnp.bfloat16)
        phase_angle = row_coord * freqs[layer_no, 0] + column_coord * freqs[layer_no, 1]
        cosine = jnp.cos(phase_angle)
        sine_part = jnp.sin(phase_angle)
        query_rot = rotate(
            jnp.dot(normed_low, query_w[layer_no], preferred_element_type=jnp.float32).reshape(
                shape_four
            ),
            cosine,
            sine_part,
        )
        key_rot = rotate(
            jnp.dot(normed_low, key_w[layer_no], preferred_element_type=jnp.float32).reshape(
                shape_four
            ),
            cosine,
            sine_part,
        )
        value_low = (
            jnp.dot(normed_low, value_w[layer_no], preferred_element_type=jnp.float32)
            .astype(jnp.bfloat16)
            .reshape(shape_four)
        )
        query_low = query_rot.astype(jnp.bfloat16)
        key_low = key_rot.astype(jnp.bfloat16)
        start_state = (
            jnp.full((images, head_count, patch_rows), MASKED_SCORE, jnp.float32),
            jnp.zeros((images, head_count, patch_rows), jnp.float32),
            jnp.zeros((images, head_count, patch_rows, head_dim), jnp.float32),
        )
        running = start_state
        held_key, held_value, held_kept = (key_low, value_low, kept_low)
        for cycle_step in range(cycle_size):
            running = merge_block(running, query_low, held_key, held_value, held_kept)
            if cycle_step + 1 < cycle_size:
                held_key, held_value, held_kept = passed_along(
                    (held_key, held_value, held_kept), "blk", 1
                )
        highest, denominator, weighted = running
        attended = (weighted / denominator[..., None]).transpose(0, 2, 1, 3)
        log_total = highest + jnp.log(denominator)
        attended_low = attended.reshape(token_rows, model_width).astype(jnp.bfloat16)
        middle = residual + jnp.dot(
            attended_low, proj_w[layer_no], preferred_element_type=jnp.float32
        )
        normed_two, norm_two_back = jax.vjp(
            layer_norm, middle, norm2_gain[layer_no], norm2_bias[layer_no]
        )
        normed_two_low = normed_two.astype(jnp.bfloat16)
        hidden = jnp.dot(normed_two_low, up_w[layer_no], preferred_element_type=jnp.float32)
        activated, gelu_back = jax.vjp(exact_gelu, hidden)
        activated_low = activated.astype(jnp.bfloat16)
        residual = middle + jnp.dot(
            activated_low, down_w[layer_no], preferred_element_type=jnp.float32
        )
        stored.append(
            (
                norm_back,
                normed_low,
                cosine,
                sine_part,
                query_rot,
                key_rot,
                query_low,
                key_low,
                value_low,
                attended,
                log_total,
                attended_low,
                norm_two_back,
                normed_two_low,
                gelu_back,
                activated_low,
            )
        )
    output = residual.astype(jnp.bfloat16).reshape(images, patch_rows, model_width)
    grad_residual = cotangent.astype(jnp.float32).reshape(token_rows, model_width)
    reduced = [None] * layer_count
    for layer_no in reversed(range(layer_count)):
        (
            norm_back,
            normed_low,
            cosine,
            sine_part,
            query_rot,
            key_rot,
            query_low,
            key_low,
            value_low,
            attended,
            log_total,
            attended_low,
            norm_two_back,
            normed_two_low,
            gelu_back,
            activated_low,
        ) = stored[layer_no]
        grad_branch = grad_residual.astype(jnp.bfloat16)
        grad_down = outer_sum(activated_low, grad_branch)
        grad_active = times_transposed(grad_branch, down_w[layer_no])
        grad_hidden = gelu_back(grad_active)[0].astype(jnp.bfloat16)
        grad_up = outer_sum(normed_two_low, grad_hidden)
        grad_middle_norm, grad_gain_two, grad_bias_two = norm_two_back(
            times_transposed(grad_hidden, up_w[layer_no])
        )
        grad_middle = grad_residual + grad_middle_norm
        grad_branch_one = grad_middle.astype(jnp.bfloat16)
        grad_proj = outer_sum(attended_low, grad_branch_one)
        grad_attended = (
            times_transposed(grad_branch_one, proj_w[layer_no])
            .astype(jnp.bfloat16)
            .reshape(shape_four)
        )
        delta_rows = jnp.sum(grad_attended.astype(jnp.float32) * attended, axis=-1).transpose(
            0, 2, 1
        )
        grad_query_rot = jnp.zeros(shape_four, jnp.float32)
        carried_key = jnp.zeros(shape_four, jnp.float32)
        carried_value = jnp.zeros(shape_four, jnp.float32)
        held_key, held_value, held_kept = (key_low, value_low, kept_low)
        for cycle_step in range(cycle_size):
            query_part, key_part, value_part = block_grads(
                query_low, grad_attended, log_total, delta_rows, held_key, held_value, held_kept
            )
            grad_query_rot = grad_query_rot + query_part
            carried_key = carried_key + key_part
            carried_value = carried_value + value_part
            if cycle_step + 1 < cycle_size:
                held_key, held_value, held_kept = passed_along(
                    (held_key, held_value, held_kept), "blk", 1
                )
            carried_key, carried_value = (
                passed_along(carried_key.astype(jnp.bfloat16), "blk", 1).astype(carried_key.dtype),
                passed_along(carried_value.astype(jnp.bfloat16), "blk", 1).astype(
                    carried_value.dtype
                ),
            )
        grad_key_rot, grad_value_sum = (carried_key, carried_value)
        angle_total = angle_grad(grad_query_rot, query_rot) + angle_grad(grad_key_rot, key_rot)
        grad_freq = jnp.stack(
            [
                jnp.sum(angle_total * row_coord, axis=(0, 1)),
                jnp.sum(angle_total * column_coord, axis=(0, 1)),
            ]
        )
        grad_query_low = (
            unrotate(grad_query_rot, cosine, sine_part)
            .astype(jnp.bfloat16)
            .reshape(token_rows, model_width)
        )
        grad_key_low = (
            unrotate(grad_key_rot, cosine, sine_part)
            .astype(jnp.bfloat16)
            .reshape(token_rows, model_width)
        )
        grad_value_low = grad_value_sum.astype(jnp.bfloat16).reshape(token_rows, model_width)
        grad_query_w = outer_sum(normed_low, grad_query_low)
        grad_key_w = outer_sum(normed_low, grad_key_low)
        grad_value_w = outer_sum(normed_low, grad_value_low)
        grad_normed = (
            times_transposed(grad_query_low, query_w[layer_no])
            + times_transposed(grad_key_low, key_w[layer_no])
            + times_transposed(grad_value_low, value_w[layer_no])
        )
        grad_input_norm, grad_gain_one, grad_bias_one = norm_back(grad_normed)
        grad_residual = grad_middle + grad_input_norm
        grads_now = (
            grad_query_w,
            grad_key_w,
            grad_value_w,
            grad_proj,
            grad_up,
            grad_down,
            grad_gain_one,
            grad_bias_one,
            grad_gain_two,
            grad_bias_two,
            grad_freq,
        )
        reduced[layer_no] = reduce_layer(grads_now)
    stacked = [
        jnp.stack([reduced[layer_no][member] for layer_no in range(layer_count)])
        for member in range(11)
    ]
    return (
        output,
        grad_residual.reshape(images, patch_rows, model_width),
        stacked[0],
        stacked[1],
        stacked[2],
        stacked[3],
        stacked[4],
        stacked[5],
        stacked[6],
        stacked[7],
        stacked[8],
        stacked[9],
        stacked[10],
    )


def solution(mesh):
    placed = (
        P("dp", "blk", None),
        P("dp", "blk"),
        P(None, "dp", "blk"),
        P(),
        P(),
        P(),
        P(),
        P(),
        P(),
        P(),
        P(),
        P(),
        P(),
        P(),
        P("dp", "blk", None),
    )
    return jax.shard_map(
        shards,
        mesh=mesh,
        in_specs=placed,
        out_specs=(
            P("dp", "blk", None),
            P("dp", "blk", None),
            P(None, "dp", "blk"),
            P(None, "dp", "blk"),
            P(None, "dp", "blk"),
            P(None, "dp", "blk"),
            P(None, "dp", "blk"),
            P(None, "dp", "blk"),
            P(None, "blk"),
            P(None, "blk"),
            P(None, "blk"),
            P(None, "blk"),
            P(None, None, "blk", None),
        ),
        check_vma=False,
    )
```

profile of v0, /device:TPU:0, one launch (start us, length us, event | category | flops | bytes accessed | tf_op | source)
XLA Modules:
  0.0 1389.1 jit_solution(11972405542199663597)
XLA Ops:
  9.5 3.2 slice_bitcast_fusion
  12.7 2.5 copy.164
  23.4 3.0 collective-permute-start.1
  31.5 2.4 copy.174
  38.7 7.6 collective-permute-done.2
  46.3 5.3 collective-permute-done.4
  53.4 12.4 collective-permute-done.3
  65.8 8.4 collective-permute-done.7
  75.1 7.6 collective-permute-done.5
  91.9 8.7 multiply_convert_fusion.9
  110.6 11.3 collective-permute-done.9
  121.9 8.3 collective-permute-done.12
  131.9 6.7 collective-permute-done.10
  138.6 8.4 collective-permute-done.13
  147.8 7.1 collective-permute-done.11
  163.2 7.8 multiply_convert_fusion.8
  181.6 3.8 fusion.110
  203.9 3.0 collective-permute-done.15
  208.4 2.6 add_convert_fusion.6
  211.0 2.6 collective-permute-start.20
  213.6 17.0 %collective-permute-done.16 = bf16[1,144,12,64]{1,3,2,0:T(8,128)(2,1)S(1)} collective-permute-done((bf16[1,144,12,64]{1,3,2,0:T(8,128)(2,1)S(1)}, bf16[1,144,12,64]{1,3,2,0:T(8,128)(2,1)S(1)}, u32[]{:S(2)}, u32[]{:S(2)}) %collective-permute-start.16) | collective-permute-done | bytes 221216 | tf_op jit(solution)/shard_map/ppermute | solution.py:14
  230.8 16.2 %collective-permute-done.20 = bf16[1,144,12,64]{1,3,2,0:T(8,128)(2,1)S(1)} collective-permute-done((bf16[1,144,12,64]{1,3,2,0:T(8,128)(2,1)S(1)}, bf16[1,144,12,64]{1,3,2,0:T(8,128)(2,1)S(1)}, u32[]{:S(2)}, u32[]{:S(2)}) %collective-permute-start.20) | collective-permute-done | bytes 221216 | tf_op jit(solution)/shard_map/ppermute | solution.py:14
  248.5 6.9 collective-permute-done.17
  255.6 8.2 collective-permute-done.21
  265.8 5.6 collective-permute-done.18
  278.9 4.4 add_convert_fusion
  289.2 2.5 convolution_convert_fusion.4
  309.7 22.7 %collective-permute-done.27 = bf16[1,144,12,64]{1,3,2,0:T(8,128)(2,1)} collective-permute-done((bf16[1,144,12,64]{1,3,2,0:T(8,128)(2,1)}, bf16[1,144,12,64]{1,3,2,0:T(8,128)(2,1)}, u32[]{:S(2)}, u32[]{:S(2)}) %collective-permute-start.27) | collective-permute-done | bytes 221216 | tf_op jit(solution)/shard_map/ppermute | solution.py:14
  332.4 2.4 add_convert_fusion.2
  337.2 18.1 %collective-permute-done.28 = bf16[1,144,12,64]{1,3,2,0:T(8,128)(2,1)S(1)} collective-permute-done((bf16[1,144,12,64]{1,3,2,0:T(8,128)(2,1)S(1)}, bf16[1,144,12,64]{1,3,2,0:T(8,128)(2,1)S(1)}, u32[]{:S(2)}, u32[]{:S(2)}) %collective-permute-start.28) | collective-permute-done | bytes 221216 | tf_op jit(solution)/shard_map/ppermute | solution.py:14
  358.0 16.5 %collective-permute-done.29 = bf16[1,144,12,64]{1,3,2,0:T(8,128)(2,1)S(1)} collective-permute-done((bf16[1,144,12,64]{1,3,2,0:T(8,128)(2,1)S(1)}, bf16[1,144,12,64]{1,3,2,0:T(8,128)(2,1)S(1)}, u32[]{:S(2)}, u32[]{:S(2)}) %collective-permute-start.29) | collective-permute-done | bytes 221216 | tf_op jit(solution)/shard_map/ppermute | solution.py:14
  378.2 14.4 %collective-permute-done.30 = bf16[1,144,12,64]{1,3,2,0:T(8,128)(2,1)S(1)} collective-permute-done((bf16[1,144,12,64]{1,3,2,0:T(8,128)(2,1)S(1)}, bf16[1,144,12,64]{1,3,2,0:T(8,128)(2,1)S(1)}, u32[]{:S(2)}, u32[]{:S(2)}) %collective-permute-start.30) | collective-permute-done | bytes 221216 | tf_op jit(solution)/shard_map/ppermute | solution.py:14
  395.0 13.0 collective-permute-done.24
  411.1 10.4 collective-permute-done.25
  423.0 16.3 %collective-permute-done.26 = bf16[1,144,12,64]{1,3,2,0:T(8,128)(2,1)S(1)} collective-permute-done((bf16[1,144,12,64]{1,3,2,0:T(8,128)(2,1)S(1)}, bf16[1,144,12,64]{1,3,2,0:T(8,128)(2,1)S(1)}, u32[]{:S(2)}, u32[]{:S(2)}) %collective-permute-start.26) | collective-permute-done | bytes 221216 | tf_op jit(solution)/shard_map/ppermute | solution.py:14
  441.6 3.9 multiply_reduce_fusion.12
  449.3 3.7 convolution_convert_fusion
  454.4 3.7 convolution_convert_fusion.1
  459.2 3.7 convolution_convert_fusion.2
  464.2 3.6 convolution_convert_fusion.3
  482.2 28.1 %reduce-scatter.45.cloned.1.call-done = bf16[768,192]{0,1:T(8,128)(2,1)} async-done(((bf16[768,768]{0,1:T(8,128)(2,1)}), bf16[768,192]{0,1:T(8,128)(2,1)}) %reduce-scatter.45.cloned.1.call-update) | async-done | bytes 294928 | tf_op jit(solution)/shard_map/reduce_scatter | solution.py:113
  512.4 28.2 %reduce-scatter.41.cloned.1.call-done = bf16[768,192]{0,1:T(8,128)(2,1)} async-done(((bf16[768,768]{0,1:T(8,128)(2,1)}), bf16[768,192]{0,1:T(8,128)(2,1)}) %reduce-scatter.41.cloned.1.call-update) | async-done | bytes 294928 | tf_op jit(solution)/shard_map/reduce_scatter | solution.py:110
  542.7 84.2 %reduce-scatter.69.cloned.1.call-done = bf16[3072,192]{0,1:T(8,128)(2,1)} async-done(((bf16[3072,768]{0,1:T(8,128)(2,1)}), bf16[3072,192]{0,1:T(8,128)(2,1)}) %reduce-scatter.69.cloned.1.call-update) | async-done | bytes 1179664 | tf_op jit(solution)/shard_map/reduce_scatter | solution.py:125
  626.9 3.0 convert_element_type.662
  630.0 84.9 %reduce-scatter.65.cloned.1.call-done = bf16[3072,192]{0,1:T(8,128)(2,1)} async-done(((bf16[3072,768]{0,1:T(8,128)(2,1)}), bf16[3072,192]{0,1:T(8,128)(2,1)}) %reduce-scatter.65.cloned.1.call-update) | async-done | bytes 1179664 | tf_op jit(solution)/shard_map/reduce_scatter | solution.py:125
  714.8 3.0 convert_element_type.660
  717.9 85.1 %reduce-scatter.61.cloned.1.call-done = bf16[768,768]{1,0:T(8,128)(2,1)} async-done(((bf16[768,3072]{1,0:T(8,128)(2,1)}), bf16[768,768]{1,0:T(8,128)(2,1)}) %reduce-scatter.61.cloned.1.call-update) | async-done | bytes 1179664 | tf_op jit(solution)/shard_map/reduce_scatter | solution.py:122
  803.0 2.8 convert_element_type.658
  808.4 4.1 fusion.137
  814.4 76.5 %reduce-scatter.57.cloned.1.call-done = bf16[768,768]{1,0:T(8,128)(2,1)} async-done(((bf16[768,3072]{1,0:T(8,128)(2,1)}), bf16[768,768]{1,0:T(8,128)(2,1)}) %reduce-scatter.57.cloned.1.call-update) | async-done | bytes 1179664 | tf_op jit(solution)/shard_map/reduce_scatter | solution.py:122
  890.9 2.9 convert_element_type.656
  897.7 18.2 %all-reduce.11 = (bf16[768]{0:T(1024)(128)(2,1)S(1)}, bf16[768]{0:T(1024)(128)(2,1)S(1)}, bf16[768]{0:T(1024)(128)(2,1)S(1)}, bf16[768]{0:T(1024)(128)(2,1)S(1)}...) all-reduce(bf16[768]{0:T(1024)(128)(2,1)S(1)} %copy-done.196, ...), channel_id=27, replica_groups=mesh['dp'=8,'blk'=4] {'blk'}, use_global_device_ids=true, to_apply=%region_62.63.clone | all-reduce | flops 7680 | bytes 30720
  916.6 22.4 %all-reduce.10 = (f32[1,192]{1,0:T(1,128)S(1)}, f32[1,192]{1,0:T(1,128)S(1)}, f32[1,192]{1,0:T(1,128)S(1)}, f32[1,192]{1,0:T(1,128)S(1)}, f32[1,192]{1,0:T(1,128...) all-reduce(f32[1,192]{1,0:T(1,128)S(1)} %bitcast.596, ...), channel_id=1, replica_groups=mesh['dp'=8,'blk'=4] {'dp'}, use_global_device_ids=true, to_apply=%region_63.64 | all-reduce | flops 1920 | bytes 15360 | tf_op jit(solution)/shard_map/psum | solution.py:152
  943.8 23.9 %reduce-scatter.85.cloned.1.call-done = f32[96,192]{1,0:T(8,128)} async-done(((f32[768,192]{1,0:T(8,128)}), f32[96,192]{1,0:T(8,128)}) %reduce-scatter.85.cloned.1.call-update) | async-done | bytes 73744
  969.6 36.2 %reduce-scatter.83.cloned.1.call-done = f32[96,192]{1,0:T(8,128)} async-done(((f32[768,192]{1,0:T(8,128)}), f32[96,192]{1,0:T(8,128)}) %reduce-scatter.83.cloned.1.call-update) | async-done | bytes 73744
  1006.8 37.0 %reduce-scatter.79.cloned.1.call-done = f32[96,192]{1,0:T(8,128)} async-done(((f32[768,192]{1,0:T(8,128)}), f32[96,192]{1,0:T(8,128)}) %reduce-scatter.79.cloned.1.call-update) | async-done | bytes 73744
  1044.8 37.0 %reduce-scatter.75.cloned.1.call-done = f32[96,192]{1,0:T(8,128)} async-done(((f32[768,192]{1,0:T(8,128)}), f32[96,192]{1,0:T(8,128)}) %reduce-scatter.75.cloned.1.call-update) | async-done | bytes 73744
  1082.8 37.0 %reduce-scatter.81.cloned.1.call-done = f32[96,192]{1,0:T(8,128)} async-done(((f32[768,192]{1,0:T(8,128)}), f32[96,192]{1,0:T(8,128)}) %reduce-scatter.81.cloned.1.call-update) | async-done | bytes 73744
  1121.7 36.4 %reduce-scatter.77.cloned.1.call-done = f32[96,192]{1,0:T(8,128)} async-done(((f32[768,192]{1,0:T(8,128)}), f32[96,192]{1,0:T(8,128)}) %reduce-scatter.77.cloned.1.call-update) | async-done | bytes 73744
  1159.8 36.2 %reduce-scatter.73.cloned.1.call-done = f32[96,192]{1,0:T(8,128)} async-done(((f32[768,192]{1,0:T(8,128)}), f32[96,192]{1,0:T(8,128)}) %reduce-scatter.73.cloned.1.call-update) | async-done | bytes 73744
  1197.9 44.1 %reduce-scatter.71.cloned.1.call-done = f32[384,192]{0,1:T(8,128)} async-done(((f32[3072,192]{0,1:T(8,128)}), f32[384,192]{0,1:T(8,128)}) %reduce-scatter.71.cloned.1.call-update) | async-done | bytes 294928 | tf_op jit(solution)/shard_map/reduce_scatter | solution.py:150
  1241.9 46.2 %reduce-scatter.67.cloned.1.call-done = f32[384,192]{0,1:T(8,128)} async-done(((f32[3072,192]{0,1:T(8,128)}), f32[384,192]{0,1:T(8,128)}) %reduce-scatter.67.cloned.1.call-update) | async-done | bytes 294928 | tf_op jit(solution)/shard_map/reduce_scatter | solution.py:150
  1290.1 44.0 %reduce-scatter.63.cloned.1.call-done = f32[96,768]{1,0:T(8,128)} async-done(((f32[768,768]{1,0:T(8,128)}), f32[96,768]{1,0:T(8,128)}) %reduce-scatter.63.cloned.1.call-update) | async-done | bytes 294928 | tf_op jit(solution)/shard_map/reduce_scatter | solution.py:149
  1334.0 46.0 %reduce-scatter.59.cloned.1.call-done = f32[96,768]{1,0:T(8,128)} async-done(((f32[768,768]{1,0:T(8,128)}), f32[96,768]{1,0:T(8,128)}) %reduce-scatter.59.cloned.1.call-update) | async-done | bytes 294928 | tf_op jit(solution)/shard_map/reduce_scatter | solution.py:149
  (735 shorter events, 186.2 us)
Async XLA Ops:
  7.2 460.8 %reduce-scatter.55.cloned.1.call-start = ((), (), s32[]{:S(2)}) async-start(), calls=%async_computation.31 | async-start | bytes 1474560 | tf_op jit(solution)/shard_map/reduce_scatter | solution.py:119
  19.1 82.9 %copy-start.144 = (f32[768]{0:T(1024)}, f32[768]{0:T(1024)S(1)}, u32[]{:S(2)}) copy-start(f32[768]{0:T(1024)S(1)} %get-tuple-element.195) | copy-start | bytes 9220
  20.4 84.3 %copy-start.148 = (f32[1,1,144]{2,1,0:T(1,128)}, f32[1,1,144]{2,1,0:T(1,128)S(1)}, u32[]{:S(2)}) copy-start(f32[1,1,144]{2,1,0:T(1,128)S(1)} %get-tuple-element.160) | copy-start | bytes 1732
  20.4 84.3 %copy-start.151 = (f32[1,1,144]{2,1,0:T(1,128)}, f32[1,1,144]{2,1,0:T(1,128)S(1)}, u32[]{:S(2)}) copy-start(f32[1,1,144]{2,1,0:T(1,128)S(1)} %get-tuple-element.161) | copy-start | bytes 1732
  22.4 60.3 %copy-start.42 = (bf16[144,12,32]{0,2,1:T(8,128)(2,1)}, bf16[144,12,32]{0,2,1:T(8,128)(2,1)S(1)}, u32[]{:S(2)}) copy-start(bf16[144,12,32]{0,2,1:T(8,128)(2,1)S(1)} %get-tuple-element.141) | copy-start | bytes 331780
  22.4 60.3 %copy-start.45 = (bf16[144,12,32]{0,2,1:T(8,128)(2,1)}, bf16[144,12,32]{0,2,1:T(8,128)(2,1)S(1)}, u32[]{:S(2)}) copy-start(bf16[144,12,32]{0,2,1:T(8,128)(2,1)S(1)} %get-tuple-element.142) | copy-start | bytes 331780
  23.4 28.3 %collective-permute-start.1 = (bf16[1,144,12,64]{1,3,2,0:T(8,128)(2,1)}, bf16[1,144,12,64]{1,3,2,0:T(8,128)(2,1)}, u32[]{:S(2)}, u32[]{:S(2)}) collective-permute-start(bf16[1,144,12,64]{1,3,2,0:T(8,128)(2,1)} %pad_maximum_fusion.4), channel_id=1, source_target_pairs={{3,0},{0,1},{1,2},{2,3},{7,4},{4,5},{5,6},{6,7},{11,8},{8,9},{9,10... | collective-permute-start | bytes 663560 | tf_op jit(solution)/shard_map/ppermute | solution.py:14
  26.4 12.3 collective-permute-start
  28.6 23.1 %collective-permute-start.6 = (bf16[1,144,12,64]{1,3,2,0:T(8,128)(2,1)S(1)}, bf16[1,144,12,64]{1,3,2,0:T(8,128)(2,1)}, u32[]{:S(2)}, u32[]{:S(2)}) collective-permute-start(bf16[1,144,12,64]{1,3,2,0:T(8,128)(2,1)S(1)} %bitcast.531), channel_id=1, source_target_pairs={{3,0},{0,1},{1,2},{2,3},{7,4},{4,5},{5,6},{6,7},{11,8},{8,9},{9,10... | collective-permute-start | bytes 663560 | tf_op jit(solution)/shard_map/ppermute | solution.py:14
  30.3 74.4 %copy-start.134 = (f32[12,32]{1,0:T(8,128)}, f32[12,32]{1,0:T(8,128)S(1)}, u32[]{:S(2)}) copy-start(f32[12,32]{1,0:T(8,128)S(1)} %get-tuple-element.196) | copy-start | bytes 4612
  30.3 74.4 %copy-start.136 = (f32[12,32]{1,0:T(8,128)}, f32[12,32]{1,0:T(8,128)S(1)}, u32[]{:S(2)}) copy-start(f32[12,32]{1,0:T(8,128)S(1)} %get-tuple-element.197) | copy-start | bytes 4612
  38.7 7.6 collective-permute-start.2
  46.3 5.4 collective-permute-start.4
  51.7 14.1 %collective-permute-start.3 = (bf16[1,144,12,64]{1,3,2,0:T(8,128)(2,1)}, bf16[1,144,12,64]{1,3,2,0:T(8,128)(2,1)S(1)}, u32[]{:S(2)}, u32[]{:S(2)}) collective-permute-start(bf16[1,144,12,64]{1,3,2,0:T(8,128)(2,1)} %collective-permute-done.1), channel_id=1, source_target_pairs={{3,0},{0,1},{1,2},{2,3},{7,4},{4,5},{5,6},{6,7},{11,8},{8,9},{9,10... | collective-permute-start | bytes 663560 | tf_op jit(solution)/shard_map/ppermute | solution.py:14
  51.8 22.5 %collective-permute-start.7 = (bf16[1,144,12,64]{1,3,2,0:T(8,128)(2,1)}, bf16[1,144,12,64]{1,3,2,0:T(8,128)(2,1)S(1)}, u32[]{:S(2)}, u32[]{:S(2)}) collective-permute-start(bf16[1,144,12,64]{1,3,2,0:T(8,128)(2,1)} %collective-permute-done.6), channel_id=1, source_target_pairs={{3,0},{0,1},{1,2},{2,3},{7,4},{4,5},{5,6},{6,7},{11,8},{8,9},{9,10... | collective-permute-start | bytes 663560 | tf_op jit(solution)/shard_map/ppermute | solution.py:14
  65.8 16.9 %collective-permute-start.5 = (bf16[1,144,12,64]{1,3,2,0:T(8,128)(2,1)S(1)}, bf16[1,144,12,64]{1,3,2,0:T(8,128)(2,1)S(1)}, u32[]{:S(2)}, u32[]{:S(2)}) collective-permute-start(bf16[1,144,12,64]{1,3,2,0:T(8,128)(2,1)S(1)} %collective-permute-done.3), channel_id=1, source_target_pairs={{3,0},{0,1},{1,2},{2,3},{7,4},{4,5},{5,6},{6,7},{11,8},{8,9},{9,10... | collective-permute-start | bytes 663560 | tf_op jit(solution)/shard_map/ppermute | solution.py:14
  74.2 14.9 %collective-permute-start.8 = (bf16[1,144,12,64]{1,3,2,0:T(8,128)(2,1)S(1)}, bf16[1,144,12,64]{1,3,2,0:T(8,128)(2,1)S(1)}, u32[]{:S(2)}, u32[]{:S(2)}) collective-permute-start(bf16[1,144,12,64]{1,3,2,0:T(8,128)(2,1)S(1)} %collective-permute-done.7), channel_id=1, source_target_pairs={{3,0},{0,1},{1,2},{2,3},{7,4},{4,5},{5,6},{6,7},{11,8},{8,9},{9,10... | collective-permute-start | bytes 663560 | tf_op jit(solution)/shard_map/ppermute | solution.py:14
  107.7 14.2 %collective-permute-start.9 = (bf16[1,144,12,64]{1,3,2,0:T(8,128)(2,1)}, bf16[1,144,12,64]{1,3,2,0:T(8,128)(2,1)}, u32[]{:S(2)}, u32[]{:S(2)}) collective-permute-start(bf16[1,144,12,64]{1,3,2,0:T(8,128)(2,1)} %pad_maximum_fusion.7), channel_id=1, source_target_pairs={{3,0},{0,1},{1,2},{2,3},{7,4},{4,5},{5,6},{6,7},{11,8},{8,9},{9,10... | collective-permute-start | bytes 663560 | tf_op jit(solution)/shard_map/ppermute | solution.py:14
  108.8 21.4 %collective-permute-start.12 = (bf16[1,144,12,64]{1,3,2,0:T(8,128)(2,1)S(1)}, bf16[1,144,12,64]{1,3,2,0:T(8,128)(2,1)S(1)}, u32[]{:S(2)}, u32[]{:S(2)}) collective-permute-start(bf16[1,144,12,64]{1,3,2,0:T(8,128)(2,1)S(1)} %bitcast.534), channel_id=1, source_target_pairs={{3,0},{0,1},{1,2},{2,3},{7,4},{4,5},{5,6},{6,7},{11,8},{8,9},{9,10... | collective-permute-start | bytes 663560 | tf_op jit(solution)/shard_map/ppermute | solution.py:14
  121.9 16.7 %collective-permute-start.10 = (bf16[1,144,12,64]{1,3,2,0:T(8,128)(2,1)}, bf16[1,144,12,64]{1,3,2,0:T(8,128)(2,1)S(1)}, u32[]{:S(2)}, u32[]{:S(2)}) collective-permute-start(bf16[1,144,12,64]{1,3,2,0:T(8,128)(2,1)} %collective-permute-done.9), channel_id=1, source_target_pairs={{3,0},{0,1},{1,2},{2,3},{7,4},{4,5},{5,6},{6,7},{11,8},{8,9},{9,10... | collective-permute-start | bytes 663560 | tf_op jit(solution)/shard_map/ppermute | solution.py:14
  130.2 16.9 %collective-permute-start.13 = (bf16[1,144,12,64]{1,3,2,0:T(8,128)(2,1)S(1)}, bf16[1,144,12,64]{1,3,2,0:T(8,128)(2,1)S(1)}, u32[]{:S(2)}, u32[]{:S(2)}) collective-permute-start(bf16[1,144,12,64]{1,3,2,0:T(8,128)(2,1)S(1)} %collective-permute-done.12), channel_id=1, source_target_pairs={{3,0},{0,1},{1,2},{2,3},{7,4},{4,5},{5,6},{6,7},{11,8},{8,9},{9,10... | collective-permute-start | bytes 663560 | tf_op jit(solution)/shard_map/ppermute | solution.py:14
  138.6 16.3 %collective-permute-start.11 = (bf16[1,144,12,64]{1,3,2,0:T(8,128)(2,1)S(1)}, bf16[1,144,12,64]{1,3,2,0:T(8,128)(2,1)S(1)}, u32[]{:S(2)}, u32[]{:S(2)}) collective-permute-start(bf16[1,144,12,64]{1,3,2,0:T(8,128)(2,1)S(1)} %collective-permute-done.10), channel_id=1, source_target_pairs={{3,0},{0,1},{1,2},{2,3},{7,4},{4,5},{5,6},{6,7},{11,8},{8,9},{9,10... | collective-permute-start | bytes 663560 | tf_op jit(solution)/shard_map/ppermute | solution.py:14
  147.1 13.3 collective-permute-start.14
  190.5 17.9 %collective-permute-start.19 = (bf16[1,144,12,64]{1,3,2,0:T(8,128)(2,1)}, bf16[1,144,12,64]{1,3,2,0:T(8,128)(2,1)}, u32[]{:S(2)}, u32[]{:S(2)}) collective-permute-start(bf16[1,144,12,64]{1,3,2,0:T(8,128)(2,1)} %fusion.110), channel_id=1, source_target_pairs={{3,0},{0,1},{1,2},{2,3},{7,4},{4,5},{5,6},{6,7},{11,8},{8,9},{9,10... | collective-permute-start | bytes 663560 | tf_op jit(solution)/shard_map/ppermute | solution.py:14
  190.5 16.4 %collective-permute-start.15 = (bf16[1,144,12,64]{1,3,2,0:T(8,128)(2,1)}, bf16[1,144,12,64]{1,3,2,0:T(8,128)(2,1)}, u32[]{:S(2)}, u32[]{:S(2)}) collective-permute-start(bf16[1,144,12,64]{1,3,2,0:T(8,128)(2,1)} %fusion.113), channel_id=1, source_target_pairs={{3,0},{0,1},{1,2},{2,3},{7,4},{4,5},{5,6},{6,7},{11,8},{8,9},{9,10... | collective-permute-start | bytes 663560 | tf_op jit(solution)/shard_map/ppermute | solution.py:14
  198.3 271.8 %reduce-scatter.53.cloned.1.call-start = ((), (), s32[]{:S(2)}) async-start(), calls=%async_computation.30 | async-start | bytes 1474560 | tf_op jit(solution)/shard_map/reduce_scatter | solution.py:119
  203.8 67.6 %copy-start.35 = (f32[1,144,12,64]{1,3,2,0:T(8,128)}, f32[1,144,12,64]{1,3,2,0:T(8,128)S(1)}, u32[]{:S(2)}) copy-start(f32[1,144,12,64]{1,3,2,0:T(8,128)S(1)} %fusion.93) | copy-start | bytes 1327108
  208.3 22.2 %collective-permute-start.16 = (bf16[1,144,12,64]{1,3,2,0:T(8,128)(2,1)S(1)}, bf16[1,144,12,64]{1,3,2,0:T(8,128)(2,1)S(1)}, u32[]{:S(2)}, u32[]{:S(2)}) collective-permute-start(bf16[1,144,12,64]{1,3,2,0:T(8,128)(2,1)S(1)} %add_convert_fusion.9), channel_id=1, source_target_pairs={{3,0},{0,1},{1,2},{2,3},{7,4},{4,5},{5,6},{6,7},{11,8},{8,9},{9,10... | collective-permute-start | bytes 663560 | tf_op jit(solution)/shard_map/ppermute | solution.py:14
  211.0 36.0 %collective-permute-start.20 = (bf16[1,144,12,64]{1,3,2,0:T(8,128)(2,1)S(1)}, bf16[1,144,12,64]{1,3,2,0:T(8,128)(2,1)S(1)}, u32[]{:S(2)}, u32[]{:S(2)}) collective-permute-start(bf16[1,144,12,64]{1,3,2,0:T(8,128)(2,1)S(1)} %add_convert_fusion.6), channel_id=1, source_target_pairs={{3,0},{0,1},{1,2},{2,3},{7,4},{4,5},{5,6},{6,7},{11,8},{8,9},{9,10... | collective-permute-start | bytes 663560 | tf_op jit(solution)/shard_map/ppermute | solution.py:14
  230.7 24.7 %collective-permute-start.17 = (bf16[1,144,12,64]{1,3,2,0:T(8,128)(2,1)S(1)}, bf16[1,144,12,64]{1,3,2,0:T(8,128)(2,1)S(1)}, u32[]{:S(2)}, u32[]{:S(2)}) collective-permute-start(bf16[1,144,12,64]{1,3,2,0:T(8,128)(2,1)S(1)} %add_convert_fusion.8), channel_id=1, source_target_pairs={{3,0},{0,1},{1,2},{2,3},{7,4},{4,5},{5,6},{6,7},{11,8},{8,9},{9,10... | collective-permute-start | bytes 663560 | tf_op jit(solution)/shard_map/ppermute | solution.py:14
  248.4 15.4 %collective-permute-start.21 = (bf16[1,144,12,64]{1,3,2,0:T(8,128)(2,1)S(1)}, bf16[1,144,12,64]{1,3,2,0:T(8,128)(2,1)S(1)}, u32[]{:S(2)}, u32[]{:S(2)}) collective-permute-start(bf16[1,144,12,64]{1,3,2,0:T(8,128)(2,1)S(1)} %fusion.101), channel_id=1, source_target_pairs={{3,0},{0,1},{1,2},{2,3},{7,4},{4,5},{5,6},{6,7},{11,8},{8,9},{9,10... | collective-permute-start | bytes 663560 | tf_op jit(solution)/shard_map/ppermute | solution.py:14
  255.6 15.8 %collective-permute-start.18 = (bf16[1,144,12,64]{1,3,2,0:T(8,128)(2,1)S(1)}, bf16[1,144,12,64]{1,3,2,0:T(8,128)(2,1)S(1)}, u32[]{:S(2)}, u32[]{:S(2)}) collective-permute-start(bf16[1,144,12,64]{1,3,2,0:T(8,128)(2,1)S(1)} %add_convert_fusion.7), channel_id=1, source_target_pairs={{3,0},{0,1},{1,2},{2,3},{7,4},{4,5},{5,6},{6,7},{11,8},{8,9},{9,10... | collective-permute-start | bytes 663560 | tf_op jit(solution)/shard_map/ppermute | solution.py:14
  265.3 10.5 collective-permute-start.22
  289.2 183.1 %reduce-scatter.51.cloned.1.call-start = ((), (), s32[]{:S(2)}) async-start(), calls=%async_computation.29 | async-start | bytes 1474560 | tf_op jit(solution)/shard_map/reduce_scatter | solution.py:116
  291.7 182.6 %reduce-scatter.47.cloned.1.call-start = ((), (), s32[]{:S(2)}) async-start(), calls=%async_computation.27 | async-start | bytes 1474560 | tf_op jit(solution)/shard_map/reduce_scatter | solution.py:113
  293.3 183.2 %reduce-scatter.43.cloned.1.call-start = ((), (), s32[]{:S(2)}) async-start(), calls=%async_computation.25 | async-start | bytes 1474560 | tf_op jit(solution)/shard_map/reduce_scatter | solution.py:110
  302.2 73.7 %collective-permute-start.23 = (bf16[1,144,12,64]{1,3,2,0:T(8,128)(2,1)}, bf16[1,144,12,64]{1,3,2,0:T(8,128)(2,1)}, u32[]{:S(2)}, u32[]{:S(2)}) collective-permute-start(bf16[1,144,12,64]{1,3,2,0:T(8,128)(2,1)} %fusion.112), channel_id=1, source_target_pairs={{3,0},{0,1},{1,2},{2,3},{7,4},{4,5},{5,6},{6,7},{11,8},{8,9},{9,10... | collective-permute-start | bytes 663560 | tf_op jit(solution)/shard_map/ppermute | solution.py:14
  304.4 28.0 %collective-permute-start.27 = (bf16[1,144,12,64]{1,3,2,0:T(8,128)(2,1)}, bf16[1,144,12,64]{1,3,2,0:T(8,128)(2,1)}, u32[]{:S(2)}, u32[]{:S(2)}) collective-permute-start(bf16[1,144,12,64]{1,3,2,0:T(8,128)(2,1)} %fusion.111), channel_id=1, source_target_pairs={{3,0},{0,1},{1,2},{2,3},{7,4},{4,5},{5,6},{6,7},{11,8},{8,9},{9,10... | collective-permute-start | bytes 663560 | tf_op jit(solution)/shard_map/ppermute | solution.py:14
  306.8 173.3 %reduce-scatter.49.cloned.1.call-start = ((), (), s32[]{:S(2)}) async-start(), calls=%async_computation.28 | async-start | bytes 1474560 | tf_op jit(solution)/shard_map/reduce_scatter | solution.py:116
  308.9 67.0 %copy-start.23 = (bf16[12,144,144]{1,2,0:T(8,128)(2,1)}, bf16[12,144,144]{1,2,0:T(8,128)(2,1)S(1)}, u32[]{:S(2)}) copy-start(bf16[12,144,144]{1,2,0:T(8,128)(2,1)S(1)} %multiply_convert_fusion.2) | copy-start | bytes 1492996
  334.8 20.4 %collective-permute-start.28 = (bf16[1,144,12,64]{1,3,2,0:T(8,128)(2,1)S(1)}, bf16[1,144,12,64]{1,3,2,0:T(8,128)(2,1)S(1)}, u32[]{:S(2)}, u32[]{:S(2)}) collective-permute-start(bf16[1,144,12,64]{1,3,2,0:T(8,128)(2,1)S(1)} %add_convert_fusion.2), channel_id=1, source_target_pairs={{3,0},{0,1},{1,2},{2,3},{7,4},{4,5},{5,6},{6,7},{11,8},{8,9},{9,10... | collective-permute-start | bytes 663560 | tf_op jit(solution)/shard_map/ppermute | solution.py:14
  356.7 17.7 %collective-permute-start.29 = (bf16[1,144,12,64]{1,3,2,0:T(8,128)(2,1)S(1)}, bf16[1,144,12,64]{1,3,2,0:T(8,128)(2,1)S(1)}, u32[]{:S(2)}, u32[]{:S(2)}) collective-permute-start(bf16[1,144,12,64]{1,3,2,0:T(8,128)(2,1)S(1)} %fusion.99), channel_id=1, source_target_pairs={{3,0},{0,1},{1,2},{2,3},{7,4},{4,5},{5,6},{6,7},{11,8},{8,9},{9,10... | collective-permute-start | bytes 663560 | tf_op jit(solution)/shard_map/ppermute | solution.py:14
  375.9 16.7 %collective-permute-start.30 = (bf16[1,144,12,64]{1,3,2,0:T(8,128)(2,1)S(1)}, bf16[1,144,12,64]{1,3,2,0:T(8,128)(2,1)S(1)}, u32[]{:S(2)}, u32[]{:S(2)}) collective-permute-start(bf16[1,144,12,64]{1,3,2,0:T(8,128)(2,1)S(1)} %fusion.98), channel_id=1, source_target_pairs={{3,0},{0,1},{1,2},{2,3},{7,4},{4,5},{5,6},{6,7},{11,8},{8,9},{9,10... | collective-permute-start | bytes 663560 | tf_op jit(solution)/shard_map/ppermute | solution.py:14
  378.1 29.9 %collective-permute-start.24 = (bf16[1,144,12,64]{1,3,2,0:T(8,128)(2,1)}, bf16[1,144,12,64]{1,3,2,0:T(8,128)(2,1)S(1)}, u32[]{:S(2)}, u32[]{:S(2)}) collective-permute-start(bf16[1,144,12,64]{1,3,2,0:T(8,128)(2,1)} %add_convert_fusion.5), channel_id=1, source_target_pairs={{3,0},{0,1},{1,2},{2,3},{7,4},{4,5},{5,6},{6,7},{11,8},{8,9},{9,10... | collective-permute-start | bytes 663560 | tf_op jit(solution)/shard_map/ppermute | solution.py:14
  395.0 115.4 %reduce-scatter.45.cloned.1.call-start = ((), (), s32[]{:S(2)}) async-start(), calls=%async_computation.26 | async-start | bytes 1474560 | tf_op jit(solution)/shard_map/reduce_scatter | solution.py:113
  409.3 12.2 collective-permute-start.25
  421.6 17.7 %collective-permute-start.26 = (bf16[1,144,12,64]{1,3,2,0:T(8,128)(2,1)S(1)}, bf16[1,144,12,64]{1,3,2,0:T(8,128)(2,1)S(1)}, u32[]{:S(2)}, u32[]{:S(2)}) collective-permute-start(bf16[1,144,12,64]{1,3,2,0:T(8,128)(2,1)S(1)} %add_convert_fusion.3), channel_id=1, source_target_pairs={{3,0},{0,1},{1,2},{2,3},{7,4},{4,5},{5,6},{6,7},{11,8},{8,9},{9,10... | collective-permute-start | bytes 663560 | tf_op jit(solution)/shard_map/ppermute | solution.py:14
  447.3 93.3 %reduce-scatter.41.cloned.1.call-start = ((), (), s32[]{:S(2)}) async-start(), calls=%async_computation.24 | async-start | bytes 1474560 | tf_op jit(solution)/shard_map/reduce_scatter | solution.py:110
  449.1 177.8 %reduce-scatter.69.cloned.1.call-start = ((), (), s32[]{:S(2)}) async-start(), calls=%async_computation.38 | async-start | bytes 5898240 | tf_op jit(solution)/shard_map/reduce_scatter | solution.py:125
  453.1 261.7 %reduce-scatter.65.cloned.1.call-start = ((), (), s32[]{:S(2)}) async-start(), calls=%async_computation.36 | async-start | bytes 5898240 | tf_op jit(solution)/shard_map/reduce_scatter | solution.py:125
  458.1 344.9 %reduce-scatter.61.cloned.1.call-start = ((), (), s32[]{:S(2)}) async-start(), calls=%async_computation.34 | async-start | bytes 5898240 | tf_op jit(solution)/shard_map/reduce_scatter | solution.py:122
  463.0 428.0 %reduce-scatter.57.cloned.1.call-start = ((), (), s32[]{:S(2)}) async-start(), calls=%async_computation.32 | async-start | bytes 5898240 | tf_op jit(solution)/shard_map/reduce_scatter | solution.py:122
  467.9 474.9 %reduce-scatter.87.cloned.1.call-start = ((), (), s32[]{:S(2)}) async-start(), calls=%async_computation.47 | async-start | bytes 884736
  470.0 497.8 %reduce-scatter.85.cloned.1.call-start = ((), (), s32[]{:S(2)}) async-start(), calls=%async_computation.46 | async-start | bytes 884736
  472.2 533.6 %reduce-scatter.83.cloned.1.call-start = ((), (), s32[]{:S(2)}) async-start(), calls=%async_computation.45 | async-start | bytes 884736
  474.3 569.5 %reduce-scatter.79.cloned.1.call-start = ((), (), s32[]{:S(2)}) async-start(), calls=%async_computation.43 | async-start | bytes 884736
  476.4 605.4 %reduce-scatter.75.cloned.1.call-start = ((), (), s32[]{:S(2)}) async-start(), calls=%async_computation.41 | async-start | bytes 884736
  478.6 641.3 %reduce-scatter.81.cloned.1.call-start = ((), (), s32[]{:S(2)}) async-start(), calls=%async_computation.44 | async-start | bytes 884736
  482.2 675.9 %reduce-scatter.77.cloned.1.call-start = ((), (), s32[]{:S(2)}) async-start(), calls=%async_computation.42 | async-start | bytes 884736
  512.4 683.7 %reduce-scatter.73.cloned.1.call-start = ((), (), s32[]{:S(2)}) async-start(), calls=%async_computation.40 | async-start | bytes 884736
  542.6 699.3 %reduce-scatter.71.cloned.1.call-start = ((), (), s32[]{:S(2)}) async-start(), calls=%async_computation.39 | async-start | bytes 2654208 | tf_op jit(solution)/shard_map/reduce_scatter | solution.py:150
  629.9 658.2 %reduce-scatter.67.cloned.1.call-start = ((), (), s32[]{:S(2)}) async-start(), calls=%async_computation.37 | async-start | bytes 2654208 | tf_op jit(solution)/shard_map/reduce_scatter | solution.py:150
  717.8 616.2 %reduce-scatter.63.cloned.1.call-start = ((), (), s32[]{:S(2)}) async-start(), calls=%async_computation.35 | async-start | bytes 2654208 | tf_op jit(solution)/shard_map/reduce_scatter | solution.py:149
  805.8 574.2 %reduce-scatter.59.cloned.1.call-start = ((), (), s32[]{:S(2)}) async-start(), calls=%async_computation.33 | async-start | bytes 2654208 | tf_op jit(solution)/shard_map/reduce_scatter | solution.py:149
  (212 other events, 1884.5 us)
Sparse Core Ops, SparseCore 0:
  198.4 48.9 reduce-scatter.54
  289.3 37.8 reduce-scatter.52
  329.5 43.1 reduce-scatter.50
  374.9 41.1 reduce-scatter.46
  418.2 31.7 reduce-scatter.42
  452.2 27.8 reduce-scatter.48
  482.4 27.8 reduce-scatter.44
  512.6 27.8 reduce-scatter.40
  542.9 83.9 reduce-scatter.68
  629.0 85.7 reduce-scatter.64
  717.2 85.7 reduce-scatter.60
  805.1 85.7 reduce-scatter.56
  894.1 35.5 reduce-scatter.86
  932.7 34.9 reduce-scatter.84
  970.8 34.9 reduce-scatter.82
  1008.8 34.9 reduce-scatter.78
  1046.8 34.9 reduce-scatter.74
  1084.8 34.9 reduce-scatter.80
  1123.0 34.9 reduce-scatter.76
  1161.0 34.9 reduce-scatter.72
  1199.4 42.5 reduce-scatter.70
  1245.6 42.4 reduce-scatter.66
  1291.5 42.4 reduce-scatter.62
  1337.6 42.4 reduce-scatter.58
where the time goes:
time: 1400 us; the launch traced here: 1390 us
  waiting for transfers between devices  1070 us (76%)
  matrix products  137 us (10%)
  local copies, waits for them, and re-layouts  67.6 us (5%)
  other arithmetic  45.1 us (3%)
  blocking collectives  40.6 us (3%)
  between operations  19.2 us (1%)
    ppermute x31, waiting for transfers between devices, passed_along(): return lax.ppermute(block, axis, route)  254 us
    unnamed x32, waiting for transfers between devices  244 us
    reduce_scatter x2, waiting for transfers between devices, reduce_layer(): lax.psum_scatter(grads[5].astype(jnp.bfloat16), 'blk', scatter_dimension=...  169 us
    reduce_scatter x2, waiting for transfers between devices, reduce_layer(): lax.psum_scatter(grads[4].astype(jnp.bfloat16), 'blk', scatter_dimension=...  162 us
    reduce_scatter x2, waiting for transfers between devices, reduce_layer(): lax.psum_scatter(shares[5], 'dp', scatter_dimension=0, tiled=True)  90.3 us
    reduce_scatter x2, waiting for transfers between devices, reduce_layer(): lax.psum_scatter(shares[4], 'dp', scatter_dimension=0, tiled=True)  90 us
    unnamed x463, local copies, waits for them, and re-layouts  46 us
    dot_general x12, matrix products, outer_sum(): lax.dot_general(left_side, right_side, (((0,), (0,)), ((), ())), preferre...  28.3 us
  transfers between devices with their start and end apart: 55, of which 42 were waited for; matrix products, arithmetic and copies ran while one was open for 12% of the time, Pallas kernels for 0%

commit v1 on v0

--- a/solution.py
+++ b/solution.py
@@ -1,6 +1,8 @@
 import jax
 import jax.numpy as jnp
 from jax import lax
+from jax.experimental import pallas as pl
+from jax.experimental.pallas import tpu as pltpu
 from jax.sharding import PartitionSpec as P
 
 MASKED_SCORE = -1e30
@@ -105,52 +107,289 @@
     return (query_part, key_part, value_part)
 
 
-def reduce_layer(grads):
-    shares = (
-        lax.psum_scatter(
-            grads[0].astype(jnp.bfloat16), "blk", scatter_dimension=1, tiled=True
-        ).astype(jnp.float32),
-        lax.psum_scatter(
-            grads[1].astype(jnp.bfloat16), "blk", scatter_dimension=1, tiled=True
-        ).astype(jnp.float32),
-        lax.psum_scatter(
-            grads[2].astype(jnp.bfloat16), "blk", scatter_dimension=1, tiled=True
-        ).astype(jnp.float32),
-        lax.psum_scatter(
-            grads[3].astype(jnp.bfloat16), "blk", scatter_dimension=1, tiled=True
-        ).astype(jnp.float32),
-        lax.psum_scatter(
-            grads[4].astype(jnp.bfloat16), "blk", scatter_dimension=1, tiled=True
-        ).astype(jnp.float32),
-        lax.psum_scatter(
-            grads[5].astype(jnp.bfloat16), "blk", scatter_dimension=1, tiled=True
-        ).astype(jnp.float32),
-        lax.psum_scatter(
-            grads[6].astype(jnp.bfloat16), "blk", scatter_dimension=0, tiled=True
-        ).astype(jnp.float32),
-        lax.psum_scatter(
-            grads[7].astype(jnp.bfloat16), "blk", scatter_dimension=0, tiled=True
-        ).astype(jnp.float32),
-        lax.psum_scatter(
-            grads[8].astype(jnp.bfloat16), "blk", scatter_dimension=0, tiled=True
-        ).astype(jnp.float32),
-        lax.psum_scatter(
-            grads[9].astype(jnp.bfloat16), "blk", scatter_dimension=0, tiled=True
-        ).astype(jnp.float32),
-        lax.psum_scatter(
-            grads[10].astype(jnp.bfloat16), "blk", scatter_dimension=1, tiled=True
-        ).astype(jnp.float32),
-    )
-    large_part = (
-        lax.psum_scatter(shares[0], "dp", scatter_dimension=0, tiled=True),
-        lax.psum_scatter(shares[1], "dp", scatter_dimension=0, tiled=True),
-        lax.psum_scatter(shares[2], "dp", scatter_dimension=0, tiled=True),
-        lax.psum_scatter(shares[3], "dp", scatter_dimension=0, tiled=True),
-        lax.psum_scatter(shares[4], "dp", scatter_dimension=0, tiled=True),
-        lax.psum_scatter(shares[5], "dp", scatter_dimension=0, tiled=True),
-    )
-    small_part = lax.psum((shares[6], shares[7], shares[8], shares[9], shares[10]), "dp")
-    return tuple(large_part) + tuple(small_part)
+MESH = pl.DeviceIdType.MESH
+PLANS = {"down": (3, 384, True), "up": (2, 576, False), "proj": (3, 96, True), "qkv": (3, 288, False)}
+
+
+class Place:
+    def __init__(self):
+        self.dp = lax.axis_index("dp")
+        self.blk = lax.axis_index("blk")
+        self.c = lax.rem(self.dp, 2)
+        self.x = lax.rem(self.dp // 2, 2)
+        self.y = lax.rem(self.dp // 4, 2)
+        self.z0 = lax.rem(self.blk, 2)
+        self.z1 = lax.rem(self.blk // 2, 2)
+
+    def other(self, axis):
+        step = {"c": 1, "x": 2, "y": 4}
+        if axis in step:
+            return (self.dp + step[axis] * (1 - 2 * getattr(self, axis)), self.blk)
+        step = {"z0": 1, "z1": 2}
+        return (self.dp, self.blk + step[axis] * (1 - 2 * getattr(self, axis)))
+
+
+def greet(place, axes):
+    barrier = pltpu.get_barrier_semaphore()
+    for axis in axes:
+        pl.semaphore_signal(barrier, inc=1, device_id=place.other(axis), device_id_type=MESH)
+    pl.semaphore_wait(barrier, len(axes))
+
+
+class Reduction:
+    def __init__(self, place, plan, share, landing, sends, receives):
+        self.place = place
+        self.n, self.rows, x_first = plan
+        self.share, self.landing = share, landing
+        self.sends, self.receives = sends, receives
+        self.first, self.second = ("x", "y") if x_first else ("y", "x")
+        n = self.n
+        self.half = 2 if n == 3 else 1
+        a, b = getattr(place, self.first), getattr(place, self.second)
+        self.offset = {}
+        self.offset[1] = ((1 - a) * 4 * n, a * 4 * n, 4 * n, 8 * n)
+        base = a * 4 * n
+        self.offset[2] = (base + (1 - b) * 2 * n, base + b * 2 * n, 2 * n, 12 * n)
+        base = base + b * 2 * n
+        self.offset[3] = (base + (1 - place.z0) * n, base + place.z0 * n, n, 14 * n)
+        base = base + place.z0 * n
+        self.offset[4] = (base + 1 - place.z1, base + place.z1, self.half, 15 * n)
+
+    def copy(self, stage):
+        send, keep, count, land = self.offset[stage]
+        axis = (None, self.first, self.second, "z0", "z1")[stage]
+        return pltpu.make_async_remote_copy(
+            src_ref=self.share.at[pl.ds(send, count)],
+            dst_ref=self.landing.at[pl.ds(land, count)],
+            send_sem=self.sends.at[stage],
+            recv_sem=self.receives.at[stage],
+            device_id=self.place.other(axis),
+            device_id_type=MESH,
+        )
+
+    def start(self, stage):
+        self.copy(stage).start()
+
+    def add(self, stage):
+        send, keep, count, land = self.offset[stage]
+        self.copy(stage).wait_recv()
+
+        def body(i, carry):
+            self.share[keep + i] = (
+                self.share[keep + i].astype(jnp.float32) + self.landing[land + i].astype(jnp.float32)
+            ).astype(jnp.bfloat16)
+            return carry
+
+        lax.fori_loop(0, count, body, 0)
+
+    def finish(self, write):
+        send, keep, count, land = self.offset[4]
+        self.copy(4).wait_recv()
+        for i in range(count):
+            write(i, self.share[keep + i].astype(jnp.float32) + self.landing[land + i].astype(jnp.float32))
+
+    def drain(self):
+        for stage in range(1, 5):
+            self.copy(stage).wait_send()
+
+
+def landing_tiles(plan):
+    n = plan[0]
+    return 15 * n + (2 if n == 3 else 1)
+
+
+def write_narrow(place, out, layer_no, rows, first_row):
+    def write(i, tile):
+        tile = tile[first_row : first_row + rows]
+
+        @pl.when(place.z1 == i)
+        def _():
+            out[layer_no, :, 0:128] = tile
+
+        @pl.when(place.z1 == 1 - i)
+        def _():
+            @pl.when(place.z1 == 0)
+            def _():
+                out[layer_no, :, 128:192] = tile[:, 0:64]
+
+            @pl.when(place.z1 == 1)
+            def _():
+                out[layer_no, :, 128:192] = tile[:, 64:128]
+
+    return write
+
+
+def reduce_kernel(layer_count, *refs):
+    names = list(PLANS)
+    count = layer_count * len(names)
+    sources = refs[:count]
+    small_in = refs[count]
+    outs = refs[count + 1 : count + 8]
+    scratch = refs[count + 8 :]
+    shares, landings = scratch[:count], scratch[count : 2 * count]
+    small, small_land, sends, receives, own_sems, small_send, small_recv = scratch[2 * count :]
+    place = Place()
+    greet(place, ("c", "x", "y", "z0", "z1"))
+    work = []
+    for index in range(count):
+        plan = PLANS[names[index % len(names)]]
+        red = Reduction(place, plan, shares[index], landings[index], sends.at[index], receives.at[index])
+        work.append(red)
+        n = plan[0]
+        pltpu.make_async_copy(sources[index].at[place.c], shares[index], own_sems.at[index]).start()
+        core_copy(red, sources[index]).start()
+    small[0] = small_in[...]
+    for index, red in enumerate(work):
+        pltpu.make_async_copy(sources[index].at[place.c], shares[index], own_sems.at[index]).wait()
+        core_copy(red, sources[index]).wait_recv()
+
+        def body(i, carry, red=red):
+            red.share[i] = (
+                red.share[i].astype(jnp.float32) + red.landing[i].astype(jnp.float32)
+            ).astype(jnp.bfloat16)
+            return carry
+
+        lax.fori_loop(0, 8 * red.n, body, 0)
+        red.start(1)
+    for stage in range(1, 4):
+        for red in work:
+            red.add(stage)
+            red.start(stage + 1)
+    for index, axis in enumerate(("c", "x", "y", "z0", "z1")):
+        copy = pltpu.make_async_remote_copy(
+            src_ref=small.at[index],
+            dst_ref=small_land.at[index],
+            send_sem=small_send.at[index],
+            recv_sem=small_recv.at[index],
+            device_id=place.other(axis),
+            device_id_type=MESH,
+        )
+        copy.start()
+        copy.wait()
+        small[index + 1] = small[index] + small_land[index]
+    outs[6][...] = small[5]
+    for index, red in enumerate(work):
+        layer_no, name = index // len(names), names[index % len(names)]
+        if name == "down":
+            red.finish(write_narrow(place, outs[5], layer_no, 384, 0))
+        elif name == "up":
+
+            def write(i, tile):
+                for part in range(6):
+                    outs[4][layer_no, :, 128 * part : 128 * part + 128] = tile[96 * part : 96 * part + 96]
+
+            red.finish(write)
+        elif name == "proj":
+            red.finish(write_narrow(place, outs[3], layer_no, 96, 0))
+        else:
+
+            def write(i, tile):
+                for part in range(3):
+                    write_narrow(place, outs[part], layer_no, 96, 96 * part)(i, tile)
+
+            red.finish(write)
+    for index, red in enumerate(work):
+        red.drain()
+        core_copy(red, sources[index]).wait_send()
+
+
+def core_copy(red, source):
+    place = red.place
+    return pltpu.make_async_remote_copy(
+        src_ref=source.at[1 - place.c],
+        dst_ref=red.landing.at[pl.ds(0, 8 * red.n)],
+        send_sem=red.sends.at[0],
+        recv_sem=red.receives.at[0],
+        device_id=place.other("c"),
+        device_id_type=MESH,
+    )
+
+
+def narrow_tiles(grad, x_first):
+    k = grad.shape[0] // 8
+    blocks = grad.reshape(2, 2, 2, k, 4, 192)
+    own = blocks[..., :128]
+    rest = blocks[..., 128:]
+    halves = []
+    for z0 in range(2):
+        shared = jnp.concatenate([rest[..., z0, :], rest[..., z0 + 2, :]], axis=-1)
+        halves.append(jnp.stack([own[..., z0, :], shared, own[..., z0 + 2, :]], axis=3))
+    tiles = jnp.stack(halves, axis=3)
+    order = (2, 1, 0, 3, 4, 5, 6) if x_first else (2, 0, 1, 3, 4, 5, 6)
+    return tiles.transpose(order)
+
+
+def wide_tiles(grad, x_first):
+    k = grad.shape[0] // 8
+    blocks = grad.reshape(2, 2, 2, k, 2, 2, 6, 128)
+    order = (2, 1, 0, 5, 4, 6, 3, 7) if x_first else (2, 0, 1, 5, 4, 6, 3, 7)
+    return blocks.transpose(order)
+
+
+def reduce_all(grads):
+    layer_count = len(grads)
+    sources = []
+    for entry in grads:
+        for name, (n, rows, x_first) in PLANS.items():
+            if name == "down":
+                tiles = narrow_tiles(entry[5].astype(jnp.bfloat16), x_first)
+            elif name == "up":
+                tiles = wide_tiles(entry[4].astype(jnp.bfloat16), x_first)
+            elif name == "proj":
+                tiles = narrow_tiles(entry[3].astype(jnp.bfloat16), x_first)
+            else:
+                tiles = jnp.concatenate(
+                    [narrow_tiles(entry[i].astype(jnp.bfloat16), x_first) for i in range(3)], axis=5
+                )
+            sources.append(tiles.reshape(2, 8 * n, rows, 128))
+    small = jnp.concatenate(
+        [
+            jnp.concatenate([jnp.stack(entry[6:10]), entry[10].reshape(1, 768), jnp.zeros((3, 768))])
+            for entry in grads
+        ]
+    ).astype(jnp.float32)
+    count = len(sources)
+    plans = [PLANS[name] for name in PLANS] * layer_count
+    sem = pltpu.SemaphoreType.DMA
+    results = pl.pallas_call(
+        lambda *refs: reduce_kernel(layer_count, *refs),
+        out_shape=[jax.ShapeDtypeStruct((layer_count, 96, 192), jnp.float32)] * 4
+        + [
+            jax.ShapeDtypeStruct((layer_count, 96, 768), jnp.float32),
+            jax.ShapeDtypeStruct((layer_count, 384, 192), jnp.float32),
+            jax.ShapeDtypeStruct(small.shape, jnp.float32),
+        ],
+        in_specs=[pl.BlockSpec(memory_space=pl.ANY)] * count + [pl.BlockSpec(memory_space=pltpu.VMEM)],
+        out_specs=[pl.BlockSpec(memory_space=pltpu.VMEM)] * 7,
+        scratch_shapes=[pltpu.VMEM((8 * plan[0], plan[1], 128), jnp.bfloat16) for plan in plans]
+        + [pltpu.VMEM((landing_tiles(plan), plan[1], 128), jnp.bfloat16) for plan in plans]
+        + [
+            pltpu.VMEM((6,) + small.shape, jnp.float32),
+            pltpu.VMEM((5,) + small.shape, jnp.float32),
+            sem((count, 5)),
+            sem((count, 5)),
+            sem((count,)),
+            sem((5,)),
+            sem((5,)),
+        ],
+        compiler_params=pltpu.CompilerParams(
+            collective_id=0, has_side_effects=True, vmem_limit_bytes=60 * 1024 * 1024
+        ),
+    )(*sources, small)
+    return results
+
+
+def beyond_eight(result):
+    dp_size = lax.axis_size("dp")
+    groups = dp_size // 8
+    if groups == 1:
+        return result
+    result = lax.psum(result, "dp", axis_index_groups=[[g * 8 + i for g in range(groups)] for i in range(8)])
+    whole = lax.all_gather(
+        result, "dp", axis=1, tiled=True, axis_index_groups=[[g * 8 + i for i in range(8)] for g in range(groups)]
+    )
+    rows = whole.shape[1] // dp_size
+    return lax.dynamic_slice_in_dim(whole, lax.axis_index("dp") * rows, rows, axis=1)
 
 
 def shards(
@@ -365,25 +604,27 @@
             grad_bias_two,
             grad_freq,
         )
-        reduced[layer_no] = reduce_layer(grads_now)
-    stacked = [
-        jnp.stack([reduced[layer_no][member] for layer_no in range(layer_count)])
-        for member in range(11)
-    ]
+        reduced[layer_no] = grads_now
+    results = reduce_all(reduced)
+    large = [beyond_eight(results[i]) for i in range(6)]
+    small = results[6].reshape(layer_count, 8, model_width)
+    if lax.axis_size("dp") > 8:
+        groups = lax.axis_size("dp") // 8
+        small = lax.psum(small, "dp", axis_index_groups=[[g * 8 + i for g in range(groups)] for i in range(8)])
+    columns = model_width // lax.axis_size("blk")
+    mine = lax.dynamic_slice_in_dim(small[:, :4], lax.axis_index("blk") * columns, columns, axis=2)
+    freq = small[:, 4].reshape(freqs.shape)
+    heads = head_count // lax.axis_size("blk")
+    freq = lax.dynamic_slice_in_dim(freq, lax.axis_index("blk") * heads, heads, axis=2)
     return (
         output,
         grad_residual.reshape(images, patch_rows, model_width),
-        stacked[0],
-        stacked[1],
-        stacked[2],
-        stacked[3],
-        stacked[4],
-        stacked[5],
-        stacked[6],
-        stacked[7],
-        stacked[8],
-        stacked[9],
-        stacked[10],
+        *large,
+        mine[:, 0],
+        mine[:, 1],
+        mine[:, 2],
+        mine[:, 3],
+        freq,
     )
 
 

time: 1400 us -> 872 us (0.62)
  waiting for transfers between devices: 1070 us -> 154 us
  local copies, waits for them, and re-layouts: 67.6 us -> 275 us
  Pallas kernels: 0 us -> 187 us
  other arithmetic: 45.1 us -> 89.7 us
  blocking collectives: 40.6 us -> 0 us
  between operations: 19.2 us -> 4.91 us
    reduce_scatter x16 -> x0, waiting for transfers between devices: 569 us -> none  [the longest x2 169 us: reduce_layer(): lax.psum_scatter(grads[5].astype(jnp.bfloat16), 'blk', scatter_dimension=...]
    unnamed x32 -> x0, waiting for transfers between devices: 244 us -> none
    pallas_call x0 -> x1, Pallas kernels: none -> 187 us  [reduce_all(): pl.pallas_call(lambda *refs: reduce_kernel(layer_count, *refs), out_shape...]
    ppermute x31, waiting for transfers between devices: 254 us -> 154 us  [passed_along(): return lax.ppermute(block, axis, route)]
    reshape x0 -> x22, local copies, waits for them, and re-layouts: none -> 77.7 us  [the longest x10 53 us: narrow_tiles(): blocks = grad.reshape(2, 2, 2, k, 4, 192)]
    slice x0 -> x19, local copies, waits for them, and re-layouts: none -> 55.8 us  [the longest x8 33 us: narrow_tiles(): shared = jnp.concatenate([rest[..., z0, :], rest[..., z0 + 2, :]], axis=-1)]
    transpose x0 -> x4, local copies, waits for them, and re-layouts: none -> 38.3 us  [the longest x2 24.6 us: narrow_tiles(): return tiles.transpose(order)]
    another operation x13 -> x42, other arithmetic: 6.82 us -> 36.2 us  [the longest x22 26.6 us: narrow_tiles(): tiles = jnp.stack(halves, axis=3)]
  transfers between devices with their start and end apart: 55 -> 31, of which waited for: 42 -> 21; matrix products, arithmetic and copies ran while one was open for 12% -> 27% of each run, Pallas kernels for 0% -> 0%
where the time goes in v1:
time: 872 us; the launch traced here: 864 us
  local copies, waits for them, and re-layouts  275 us (32%)
  Pallas kernels  187 us (21%)
  waiting for transfers between devices  154 us (18%)
  matrix products  134 us (15%)
  other arithmetic  89.7 us (10%)
  starting transfers between devices  19.8 us (2%)
    pallas_call x1, Pallas kernels, reduce_all(): pl.pallas_call(lambda *refs: reduce_kernel(layer_count, *refs), out_shape...  187 us
    ppermute x31, waiting for transfers between devices, passed_along(): return lax.ppermute(block, axis, route)  154 us
    unnamed x766, local copies, waits for them, and re-layouts  57 us
    reshape x10, local copies, waits for them, and re-layouts, narrow_tiles(): blocks = grad.reshape(2, 2, 2, k, 4, 192)  53 us
    slice x8, local copies, waits for them, and re-layouts, narrow_tiles(): shared = jnp.concatenate([rest[..., z0, :], rest[..., z0 + 2, :]], axis=-1)  33 us
    another operation x22, other arithmetic, narrow_tiles(): tiles = jnp.stack(halves, axis=3)  26.6 us
    dot_general x12, matrix products, outer_sum(): lax.dot_general(left_side, right_side, (((0,), (0,)), ((), ())), preferre...  26.4 us
    transpose x2, local copies, waits for them, and re-layouts, narrow_tiles(): return tiles.transpose(order)  24.6 us
  transfers between devices with their start and end apart: 31, of which 21 were waited for; matrix products, arithmetic and copies ran while one was open for 27% of the time, Pallas kernels for 0%

profile of v1, /device:TPU:0, one launch (start us, length us, event | category | flops | bytes accessed | tf_op | source)
XLA Modules:
  0.0 863.8 jit_solution(6537134018803481384)
XLA Ops:
  3.5 2.8 slice_bitcast_fusion
  15.8 3.0 collective-permute-start.1
  31.2 7.5 collective-permute-done.2
  38.8 5.3 collective-permute-done.4
  45.9 12.3 %collective-permute-done.3 = bf16[1,144,12,64]{1,3,2,0:T(8,128)(2,1)S(1)} collective-permute-done((bf16[1,144,12,64]{1,3,2,0:T(8,128)(2,1)}, bf16[1,144,12,64]{1,3,2,0:T(8,128)(2,1)S(1)}, u32[]{:S(2)}, u32[]{:S(2)}) %collective-permute-start.3) | collective-permute-done | bytes 221216 | tf_op jit(solution)/shard_map/ppermute | solution.py:16
  58.3 8.4 collective-permute-done.7
  67.6 7.6 collective-permute-done.5
  83.4 8.6 %multiply_convert_fusion.9 = (bf16[144,3072]{1,0:T(8,128)(2,1)S(1)}, f32[144,3072]{1,0:T(8,128)}, f32[144,3072]{1,0:T(8,128)}) fusion(bf16[2,768,3072]{2,1,0:T(8,128)(2,1)} %param.22, f32[144,768]{1,0:T(8,128)S(1)} %get-tuple-element.238, f32[768]{0:T(1024)S(1)} %get-tuple-element.73, f32[768]{0:T(1024)S(1)} %get-tuple-element.265, f32[144]{0:T(256)S(1)} %fusion.259, ...), kind=kOutput, calls=%fused_computation.79 | convolution fusion | flops 708784128 | bytes 9591936 | tf_op jit(solution)/shard_map/dot_general | solution.py:477
  101.9 11.3 %collective-permute-done.9 = bf16[1,144,12,64]{1,3,2,0:T(8,128)(2,1)} collective-permute-done((bf16[1,144,12,64]{1,3,2,0:T(8,128)(2,1)}, bf16[1,144,12,64]{1,3,2,0:T(8,128)(2,1)}, u32[]{:S(2)}, u32[]{:S(2)}) %collective-permute-start.9) | collective-permute-done | bytes 221216 | tf_op jit(solution)/shard_map/ppermute | solution.py:16
  113.2 8.3 collective-permute-done.12
  123.3 6.7 collective-permute-done.10
  130.0 8.4 collective-permute-done.13
  139.1 7.7 collective-permute-done.11
  155.1 7.8 multiply_convert_fusion.8
  173.5 3.8 fusion.110
  182.3 4.8 reshape.1665
  187.2 5.0 fusion.312
  194.8 3.7 convolution_convert_fusion.1
  198.6 6.7 copy.271
  205.2 11.6 %reshape.1661 = bf16[2,2,2,384,4,192]{3,2,1,0,5,4:T(2,128)(2,1)} reshape(bf16[3072,768]{0,1:T(8,128)(2,1)} %copy.271) | data formatting | bytes 9437184 | tf_op jit(solution)/shard_map/reshape | solution.py:310
  219.3 3.6 slice_bitcast_fusion.7
  223.0 3.6 convolution_convert_fusion
  226.7 4.0 fusion.137
  243.3 5.1 maximum_bitcast_fusion.4
  248.4 4.9 maximum_bitcast_fusion.5
  253.2 11.6 %maximum_bitcast_fusion.1 = bf16[2,2,2,2,3,384,128]{5,0,1,2,6,4,3:T(2,128)(2,1)} fusion(bf16[2,2,2,1,3,384,128]{5,2,1,0,6,4,3:T(2,128)(2,1)} %maximum_bitcast_fusion.5, bf16[2,2,2,1,3,384,128]{5,2,1,0,6,4,3:T(2,128)(2,1)} %maximum_bitcast_fusion.4), kind=kLoop, calls=%fused_computation.5 | loop fusion | flops 2359296 | bytes 9437184 | tf_op jit(solution)/shard_map/transpose | solution.py:319
  273.7 12.3 %copy.272 = bf16[2,2,2,2,3,384,128]{6,5,4,3,2,1,0:T(8,128)(2,1)} copy(bf16[2,2,2,2,3,384,128]{5,0,1,2,6,4,3:T(2,128)(2,1)} %maximum_bitcast_fusion.1) | data formatting | bytes 9437184 | tf_op jit(solution)/shard_map/transpose | solution.py:319
  286.0 10.6 %reshape.1663 = bf16[2,2,2,96,2,2,6,128]{7,6,5,4,3,2,1,0:T(8,128)(2,1)} reshape(bf16[768,3072]{1,0:T(8,128)(2,1)} %convolution_convert_fusion) | data formatting | bytes 9437184 | tf_op jit(solution)/shard_map/reshape | solution.py:324
  296.7 6.9 copy.273
  309.3 4.2 collective-permute-start.20
  313.5 6.5 collective-permute-done.16
  320.8 7.6 collective-permute-done.20
  330.6 6.3 collective-permute-done.17
  337.7 7.6 collective-permute-done.21
  347.4 4.9 collective-permute-done.18
  360.3 4.4 add_convert_fusion
  381.4 4.5 reshape.1667
  385.9 5.0 fusion.306
  395.2 4.4 reshape.1668
  399.6 5.0 fusion.308
  408.9 4.6 reshape.1669
  413.5 5.0 fusion.310
  422.7 4.4 reshape.1655
  427.1 5.0 fusion.320
  434.8 3.6 convolution_convert_fusion.2
  438.4 3.6 convolution_convert_fusion.3
  442.1 6.6 copy.236
  448.7 12.1 %reshape.1651 = bf16[2,2,2,384,4,192]{3,2,1,0,5,4:T(2,128)(2,1)} reshape(bf16[3072,768]{0,1:T(8,128)(2,1)} %copy.236) | data formatting | bytes 9437184 | tf_op jit(solution)/shard_map/reshape | solution.py:310
  460.8 3.4 slice_bitcast_fusion.19
  464.2 4.6 slice_bitcast_fusion.11
  501.3 10.4 %reshape.1653 = bf16[2,2,2,96,2,2,6,128]{7,6,5,4,3,2,1,0:T(8,128)(2,1)} reshape(bf16[768,3072]{1,0:T(8,128)(2,1)} %convolution_convert_fusion.2) | data formatting | bytes 9437184 | tf_op jit(solution)/shard_map/reshape | solution.py:324
  511.7 6.8 copy.238
  520.7 4.9 maximum_bitcast_fusion.2
  525.6 5.0 maximum_bitcast_fusion.3
  530.7 11.6 %maximum_bitcast_fusion = bf16[2,2,2,2,3,384,128]{5,0,1,2,6,4,3:T(2,128)(2,1)} fusion(bf16[2,2,2,1,3,384,128]{5,2,1,0,6,4,3:T(2,128)(2,1)} %maximum_bitcast_fusion.3, bf16[2,2,2,1,3,384,128]{5,2,1,0,6,4,3:T(2,128)(2,1)} %maximum_bitcast_fusion.2), kind=kLoop, calls=%fused_computation.4 | loop fusion | flops 2359296 | bytes 9437184 | tf_op jit(solution)/shard_map/transpose | solution.py:319
  542.2 12.3 %copy.237 = bf16[2,2,2,2,3,384,128]{6,5,4,3,2,1,0:T(8,128)(2,1)} copy(bf16[2,2,2,2,3,384,128]{5,0,1,2,6,4,3:T(2,128)(2,1)} %maximum_bitcast_fusion) | data formatting | bytes 9437184 | tf_op jit(solution)/shard_map/transpose | solution.py:319
  577.1 9.0 %collective-permute-done.24 = bf16[1,144,12,64]{1,3,2,0:T(8,128)(2,1)S(1)} collective-permute-done((bf16[1,144,12,64]{1,3,2,0:T(8,128)(2,1)S(1)}, bf16[1,144,12,64]{1,3,2,0:T(8,128)(2,1)S(1)}, u32[]{:S(2)}, u32[]{:S(2)}) %collective-permute-start.24) | collective-permute-done | bytes 221216 | tf_op jit(solution)/shard_map/ppermute | solution.py:16
  586.3 8.2 collective-permute-done.28
  596.0 6.9 collective-permute-done.25
  603.2 8.2 collective-permute-done.29
  616.1 2.8 subtract_add_fusion.1
  620.7 3.5 reshape.1657
  629.5 3.9 multiply_reduce_fusion.14
  665.2 186.9 %shard_map.246 = (f32[2,96,192]{2,1,0:T(8,128)}, f32[2,96,192]{2,1,0:T(8,128)}, f32[2,96,192]{2,1,0:T(8,128)}, f32[2,96,192]{2,1,0:T(8,128)}, f32[2,96,768]{2,1,...) custom-call(bf16[2,24,384,128]{3,2,1,0:T(8,128)(2,1)} %bitcast.838, bf16[2,16,576,128]{3,2,1,0:T(8,128)(2,1)} %bitcast.840, ...), custom_call_target="tpu_custom_call" | custom-call | tf_op jit(solution)/shard_map/pallas_call | solution.py:354
  (1045 shorter events, 260.6 us)
Async XLA Ops:
  1.7 18.8 %copy-start.262 = (f32[144]{0:T(256)}, f32[144]{0:T(256)S(1)}, u32[]{:S(2)}) copy-start(f32[144]{0:T(256)S(1)} %broadcast_multiply_fusion.3) | copy-start | bytes 1732
  3.5 17.0 %copy-start.266 = (f32[144]{0:T(256)}, f32[144]{0:T(256)S(1)}, u32[]{:S(2)}) copy-start(f32[144]{0:T(256)S(1)} %fusion.258) | copy-start | bytes 1732
  15.0 60.1 %copy-start.53 = (bf16[144,12,32]{0,2,1:T(8,128)(2,1)}, bf16[144,12,32]{0,2,1:T(8,128)(2,1)S(1)}, u32[]{:S(2)}) copy-start(bf16[144,12,32]{0,2,1:T(8,128)(2,1)S(1)} %get-tuple-element.203) | copy-start | bytes 331780
  15.0 361.4 %copy-start.50 = (bf16[144,12,32]{0,2,1:T(8,128)(2,1)}, bf16[144,12,32]{0,2,1:T(8,128)(2,1)S(1)}, u32[]{:S(2)}) copy-start(bf16[144,12,32]{0,2,1:T(8,128)(2,1)S(1)} %get-tuple-element.202) | copy-start | bytes 331780
  15.8 28.3 %collective-permute-start.1 = (bf16[1,144,12,64]{1,3,2,0:T(8,128)(2,1)}, bf16[1,144,12,64]{1,3,2,0:T(8,128)(2,1)}, u32[]{:S(2)}, u32[]{:S(2)}) collective-permute-start(bf16[1,144,12,64]{1,3,2,0:T(8,128)(2,1)} %pad_maximum_fusion.6), channel_id=1, source_target_pairs={{3,0},{0,1},{1,2},{2,3},{7,4},{4,5},{5,6},{6,7},{11,8},{8,9},{9,10... | collective-permute-start | bytes 663560 | tf_op jit(solution)/shard_map/ppermute | solution.py:16
  18.9 12.3 %collective-permute-start = (bf16[1,144]{1,0:T(2,128)(2,1)S(1)}, bf16[1,144]{1,0:T(2,128)(2,1)S(1)}, u32[]{:S(2)}, u32[]{:S(2)}) collective-permute-start(bf16[1,144]{1,0:T(2,128)(2,1)S(1)} %convert_element_type.466), channel_id=1, source_target_pairs={{3,0},{0,1},{1,2},{2,3},{7,4},{4,5},{5,6},{6,7},{11,8},{8,9},{9,10... | collective-permute-start | bytes 872 | tf_op jit(solution)/shard_map/ppermute | solution.py:16
  21.1 56.2 %copy-start.74 = (bf16[144,768]{0,1:T(8,128)(2,1)}, bf16[144,768]{0,1:T(8,128)(2,1)S(1)}, u32[]{:S(2)}) copy-start(bf16[144,768]{0,1:T(8,128)(2,1)S(1)} %copy.184) | copy-start | bytes 663556
  21.1 23.1 %collective-permute-start.6 = (bf16[1,144,12,64]{1,3,2,0:T(8,128)(2,1)S(1)}, bf16[1,144,12,64]{1,3,2,0:T(8,128)(2,1)S(1)}, u32[]{:S(2)}, u32[]{:S(2)}) collective-permute-start(bf16[1,144,12,64]{1,3,2,0:T(8,128)(2,1)S(1)} %bitcast.851), channel_id=1, source_target_pairs={{3,0},{0,1},{1,2},{2,3},{7,4},{4,5},{5,6},{6,7},{11,8},{8,9},{9,10... | collective-permute-start | bytes 663560 | tf_op jit(solution)/shard_map/ppermute | solution.py:16
  22.8 54.5 %copy-start.272 = (pred[144]{0:T(512)(128)(4,1)}, pred[144]{0:T(512)(128)(4,1)S(1)}, u32[]{:S(2)}) copy-start(pred[144]{0:T(512)(128)(4,1)S(1)} %compare_reduce_fusion.3) | copy-start | bytes 436
  31.2 7.6 collective-permute-start.2
  31.2 47.1 %copy-start.282 = (pred[144]{0:T(512)(128)(4,1)}, pred[144]{0:T(512)(128)(4,1)S(1)}, u32[]{:S(2)}) copy-start(pred[144]{0:T(512)(128)(4,1)S(1)} %compare_reduce_fusion.2) | copy-start | bytes 436
  38.7 5.4 collective-permute-start.4
  38.8 40.7 %copy-start.278 = (pred[144]{0:T(512)(128)(4,1)}, pred[144]{0:T(512)(128)(4,1)S(1)}, u32[]{:S(2)}) copy-start(pred[144]{0:T(512)(128)(4,1)S(1)} %compare_reduce_fusion.1) | copy-start | bytes 436
  44.1 36.5 %copy-start.295 = (pred[144]{0:T(512)(128)(4,1)}, pred[144]{0:T(512)(128)(4,1)S(1)}, u32[]{:S(2)}) copy-start(pred[144]{0:T(512)(128)(4,1)S(1)} %compare_reduce_fusion) | copy-start | bytes 436
  44.1 14.1 %collective-permute-start.3 = (bf16[1,144,12,64]{1,3,2,0:T(8,128)(2,1)}, bf16[1,144,12,64]{1,3,2,0:T(8,128)(2,1)S(1)}, u32[]{:S(2)}, u32[]{:S(2)}) collective-permute-start(bf16[1,144,12,64]{1,3,2,0:T(8,128)(2,1)} %collective-permute-done.1), channel_id=1, source_target_pairs={{3,0},{0,1},{1,2},{2,3},{7,4},{4,5},{5,6},{6,7},{11,8},{8,9},{9,10... | collective-permute-start | bytes 663560 | tf_op jit(solution)/shard_map/ppermute | solution.py:16
  44.2 23.3 %copy-start.192 = (bf16[1,144,12,64]{1,3,2,0:T(8,128)(2,1)}, bf16[1,144,12,64]{1,3,2,0:T(8,128)(2,1)S(1)}, u32[]{:S(2)}) copy-start(bf16[1,144,12,64]{1,3,2,0:T(8,128)(2,1)S(1)} %collective-permute-done.6) | copy-start | bytes 663556
  44.2 22.5 %collective-permute-start.7 = (bf16[1,144,12,64]{1,3,2,0:T(8,128)(2,1)S(1)}, bf16[1,144,12,64]{1,3,2,0:T(8,128)(2,1)S(1)}, u32[]{:S(2)}, u32[]{:S(2)}) collective-permute-start(bf16[1,144,12,64]{1,3,2,0:T(8,128)(2,1)S(1)} %collective-permute-done.6), channel_id=1, source_target_pairs={{3,0},{0,1},{1,2},{2,3},{7,4},{4,5},{5,6},{6,7},{11,8},{8,9},{9,10... | collective-permute-start | bytes 663560 | tf_op jit(solution)/shard_map/ppermute | solution.py:16
  45.9 32.4 %copy-start = (f32[12,144,144]{1,2,0:T(8,128)}, f32[12,144,144]{1,2,0:T(8,128)S(1)}, u32[]{:S(2)}) copy-start(f32[12,144,144]{1,2,0:T(8,128)S(1)} %get-tuple-element.232) | copy-start | bytes 2985988
  58.3 16.9 %collective-permute-start.5 = (bf16[1,144,12,64]{1,3,2,0:T(8,128)(2,1)S(1)}, bf16[1,144,12,64]{1,3,2,0:T(8,128)(2,1)S(1)}, u32[]{:S(2)}, u32[]{:S(2)}) collective-permute-start(bf16[1,144,12,64]{1,3,2,0:T(8,128)(2,1)S(1)} %collective-permute-done.3), channel_id=1, source_target_pairs={{3,0},{0,1},{1,2},{2,3},{7,4},{4,5},{5,6},{6,7},{11,8},{8,9},{9,10... | collective-permute-start | bytes 663560 | tf_op jit(solution)/shard_map/ppermute | solution.py:16
  66.7 13.9 %collective-permute-start.8 = (bf16[1,144,12,64]{1,3,2,0:T(8,128)(2,1)S(1)}, bf16[1,144,12,64]{1,3,2,0:T(8,128)(2,1)S(1)}, u32[]{:S(2)}, u32[]{:S(2)}) collective-permute-start(bf16[1,144,12,64]{1,3,2,0:T(8,128)(2,1)S(1)} %collective-permute-done.7), channel_id=1, source_target_pairs={{3,0},{0,1},{1,2},{2,3},{7,4},{4,5},{5,6},{6,7},{11,8},{8,9},{9,10... | collective-permute-start | bytes 663560 | tf_op jit(solution)/shard_map/ppermute | solution.py:16
  98.1 48.8 %copy-start.57 = (bf16[144,12,32]{0,2,1:T(8,128)(2,1)}, bf16[144,12,32]{0,2,1:T(8,128)(2,1)S(1)}, u32[]{:S(2)}) copy-start(bf16[144,12,32]{0,2,1:T(8,128)(2,1)S(1)} %get-tuple-element.198) | copy-start | bytes 331780
  98.1 48.7 %copy-start.60 = (bf16[144,12,32]{0,2,1:T(8,128)(2,1)}, bf16[144,12,32]{0,2,1:T(8,128)(2,1)S(1)}, u32[]{:S(2)}) copy-start(bf16[144,12,32]{0,2,1:T(8,128)(2,1)S(1)} %get-tuple-element.199) | copy-start | bytes 331780
  99.0 22.5 %copy-start.283 = (pred[144]{0:T(512)(128)(4,1)S(1)}, pred[144]{0:T(512)(128)(4,1)}, u32[]{:S(2)}) copy-start(pred[144]{0:T(512)(128)(4,1)} %copy-done.282) | copy-start | bytes 436
  99.0 14.2 %collective-permute-start.9 = (bf16[1,144,12,64]{1,3,2,0:T(8,128)(2,1)}, bf16[1,144,12,64]{1,3,2,0:T(8,128)(2,1)}, u32[]{:S(2)}, u32[]{:S(2)}) collective-permute-start(bf16[1,144,12,64]{1,3,2,0:T(8,128)(2,1)} %pad_maximum_fusion.9), channel_id=1, source_target_pairs={{3,0},{0,1},{1,2},{2,3},{7,4},{4,5},{5,6},{6,7},{11,8},{8,9},{9,10... | collective-permute-start | bytes 663560 | tf_op jit(solution)/shard_map/ppermute | solution.py:16
  100.2 48.8 %copy-start.75 = (bf16[144,768]{0,1:T(8,128)(2,1)}, bf16[144,768]{0,1:T(8,128)(2,1)S(1)}, u32[]{:S(2)}) copy-start(bf16[144,768]{0,1:T(8,128)(2,1)S(1)} %copy.194) | copy-start | bytes 663556
  100.2 21.4 %collective-permute-start.12 = (bf16[1,144,12,64]{1,3,2,0:T(8,128)(2,1)S(1)}, bf16[1,144,12,64]{1,3,2,0:T(8,128)(2,1)S(1)}, u32[]{:S(2)}, u32[]{:S(2)}) collective-permute-start(bf16[1,144,12,64]{1,3,2,0:T(8,128)(2,1)S(1)} %bitcast.854), channel_id=1, source_target_pairs={{3,0},{0,1},{1,2},{2,3},{7,4},{4,5},{5,6},{6,7},{11,8},{8,9},{9,10... | collective-permute-start | bytes 663560 | tf_op jit(solution)/shard_map/ppermute | solution.py:16
  101.9 47.1 %copy-start.10 = (f32[12,144,144]{1,2,0:T(8,128)}, f32[12,144,144]{1,2,0:T(8,128)S(1)}, u32[]{:S(2)}) copy-start(f32[12,144,144]{1,2,0:T(8,128)S(1)} %get-tuple-element.249) | copy-start | bytes 2985988
  101.9 36.7 %copy-start.279 = (pred[144]{0:T(512)(128)(4,1)S(1)}, pred[144]{0:T(512)(128)(4,1)}, u32[]{:S(2)}) copy-start(pred[144]{0:T(512)(128)(4,1)} %copy-done.278) | copy-start | bytes 436
  113.2 16.7 %collective-permute-start.10 = (bf16[1,144,12,64]{1,3,2,0:T(8,128)(2,1)}, bf16[1,144,12,64]{1,3,2,0:T(8,128)(2,1)S(1)}, u32[]{:S(2)}, u32[]{:S(2)}) collective-permute-start(bf16[1,144,12,64]{1,3,2,0:T(8,128)(2,1)} %collective-permute-done.9), channel_id=1, source_target_pairs={{3,0},{0,1},{1,2},{2,3},{7,4},{4,5},{5,6},{6,7},{11,8},{8,9},{9,10... | collective-permute-start | bytes 663560 | tf_op jit(solution)/shard_map/ppermute | solution.py:16
  121.5 28.5 %copy-start.197 = (bf16[1,144,12,64]{1,3,2,0:T(8,128)(2,1)}, bf16[1,144,12,64]{1,3,2,0:T(8,128)(2,1)S(1)}, u32[]{:S(2)}) copy-start(bf16[1,144,12,64]{1,3,2,0:T(8,128)(2,1)S(1)} %collective-permute-done.12) | copy-start | bytes 663556
  121.5 16.9 %collective-permute-start.13 = (bf16[1,144,12,64]{1,3,2,0:T(8,128)(2,1)S(1)}, bf16[1,144,12,64]{1,3,2,0:T(8,128)(2,1)S(1)}, u32[]{:S(2)}, u32[]{:S(2)}) collective-permute-start(bf16[1,144,12,64]{1,3,2,0:T(8,128)(2,1)S(1)} %collective-permute-done.12), channel_id=1, source_target_pairs={{3,0},{0,1},{1,2},{2,3},{7,4},{4,5},{5,6},{6,7},{11,8},{8,9},{9,10... | collective-permute-start | bytes 663560 | tf_op jit(solution)/shard_map/ppermute | solution.py:16
  123.2 26.9 %copy-start.7 = (f32[12,144,144]{1,2,0:T(8,128)}, f32[12,144,144]{1,2,0:T(8,128)S(1)}, u32[]{:S(2)}) copy-start(f32[12,144,144]{1,2,0:T(8,128)S(1)} %get-tuple-element.247) | copy-start | bytes 2985988
  123.2 23.6 %copy-start.296 = (pred[144]{0:T(512)(128)(4,1)S(1)}, pred[144]{0:T(512)(128)(4,1)}, u32[]{:S(2)}) copy-start(pred[144]{0:T(512)(128)(4,1)} %copy-done.295) | copy-start | bytes 436
  130.0 17.4 %copy-start.248 = (bf16[1,144,12,64]{1,3,2,0:T(8,128)(2,1)}, bf16[1,144,12,64]{1,3,2,0:T(8,128)(2,1)S(1)}, u32[]{:S(2)}) copy-start(bf16[1,144,12,64]{1,3,2,0:T(8,128)(2,1)S(1)} %collective-permute-done.10) | copy-start | bytes 663556
  130.0 16.9 %collective-permute-start.11 = (bf16[1,144,12,64]{1,3,2,0:T(8,128)(2,1)S(1)}, bf16[1,144,12,64]{1,3,2,0:T(8,128)(2,1)S(1)}, u32[]{:S(2)}, u32[]{:S(2)}) collective-permute-start(bf16[1,144,12,64]{1,3,2,0:T(8,128)(2,1)S(1)} %collective-permute-done.10), channel_id=1, source_target_pairs={{3,0},{0,1},{1,2},{2,3},{7,4},{4,5},{5,6},{6,7},{11,8},{8,9},{9,10... | collective-permute-start | bytes 663560 | tf_op jit(solution)/shard_map/ppermute | solution.py:16
  138.4 13.9 %collective-permute-start.14 = (bf16[1,144,12,64]{1,3,2,0:T(8,128)(2,1)S(1)}, bf16[1,144,12,64]{1,3,2,0:T(8,128)(2,1)S(1)}, u32[]{:S(2)}, u32[]{:S(2)}) collective-permute-start(bf16[1,144,12,64]{1,3,2,0:T(8,128)(2,1)S(1)} %collective-permute-done.13), channel_id=1, source_target_pairs={{3,0},{0,1},{1,2},{2,3},{7,4},{4,5},{5,6},{6,7},{11,8},{8,9},{9,10... | collective-permute-start | bytes 663560 | tf_op jit(solution)/shard_map/ppermute | solution.py:16
  230.7 76.1 %collective-permute-start.19 = (bf16[1,144,12,64]{1,3,2,0:T(8,128)(2,1)}, bf16[1,144,12,64]{1,3,2,0:T(8,128)(2,1)}, u32[]{:S(2)}, u32[]{:S(2)}) collective-permute-start(bf16[1,144,12,64]{1,3,2,0:T(8,128)(2,1)} %fusion.110), channel_id=1, source_target_pairs={{3,0},{0,1},{1,2},{2,3},{7,4},{4,5},{5,6},{6,7},{11,8},{8,9},{9,10... | collective-permute-start | bytes 663560 | tf_op jit(solution)/shard_map/ppermute | solution.py:16
  230.7 73.1 %collective-permute-start.15 = (bf16[1,144,12,64]{1,3,2,0:T(8,128)(2,1)}, bf16[1,144,12,64]{1,3,2,0:T(8,128)(2,1)}, u32[]{:S(2)}, u32[]{:S(2)}) collective-permute-start(bf16[1,144,12,64]{1,3,2,0:T(8,128)(2,1)} %fusion.113), channel_id=1, source_target_pairs={{3,0},{0,1},{1,2},{2,3},{7,4},{4,5},{5,6},{6,7},{11,8},{8,9},{9,10... | collective-permute-start | bytes 663560 | tf_op jit(solution)/shard_map/ppermute | solution.py:16
  303.8 48.5 %copy-start.43 = (f32[1,144,12,64]{1,3,2,0:T(8,128)}, f32[1,144,12,64]{1,3,2,0:T(8,128)S(1)}, u32[]{:S(2)}) copy-start(f32[1,144,12,64]{1,3,2,0:T(8,128)S(1)} %fusion.93) | copy-start | bytes 1327108
  306.1 13.9 %copy-start.92 = (f32[1,144,12,64]{1,3,2,0:T(8,128)S(1)}, f32[1,144,12,64]{1,3,2,0:T(8,128)}, u32[]{:S(2)}) copy-start(f32[1,144,12,64]{1,3,2,0:T(8,128)} %fusion.90) | copy-start | bytes 1327108
  306.1 22.3 %copy-start.6 = (f32[12,144,144]{1,2,0:T(8,128)S(1)}, f32[12,144,144]{1,2,0:T(8,128)}, u32[]{:S(2)}) copy-start(f32[12,144,144]{1,2,0:T(8,128)} %copy-done.4) | copy-start | bytes 2985988
  306.1 13.9 %collective-permute-start.16 = (bf16[1,144,12,64]{1,3,2,0:T(8,128)(2,1)S(1)}, bf16[1,144,12,64]{1,3,2,0:T(8,128)(2,1)S(1)}, u32[]{:S(2)}, u32[]{:S(2)}) collective-permute-start(bf16[1,144,12,64]{1,3,2,0:T(8,128)(2,1)S(1)} %add_convert_fusion.9), channel_id=1, source_target_pairs={{3,0},{0,1},{1,2},{2,3},{7,4},{4,5},{5,6},{6,7},{11,8},{8,9},{9,10... | collective-permute-start | bytes 663560 | tf_op jit(solution)/shard_map/ppermute | solution.py:16
  309.3 19.2 %collective-permute-start.20 = (bf16[1,144,12,64]{1,3,2,0:T(8,128)(2,1)S(1)}, bf16[1,144,12,64]{1,3,2,0:T(8,128)(2,1)S(1)}, u32[]{:S(2)}, u32[]{:S(2)}) collective-permute-start(bf16[1,144,12,64]{1,3,2,0:T(8,128)(2,1)S(1)} %add_convert_fusion.6), channel_id=1, source_target_pairs={{3,0},{0,1},{1,2},{2,3},{7,4},{4,5},{5,6},{6,7},{11,8},{8,9},{9,10... | collective-permute-start | bytes 663560 | tf_op jit(solution)/shard_map/ppermute | solution.py:16
  320.2 16.7 %copy-start.91 = (f32[1,144,12,64]{1,3,2,0:T(8,128)S(1)}, f32[1,144,12,64]{1,3,2,0:T(8,128)}, u32[]{:S(2)}) copy-start(f32[1,144,12,64]{1,3,2,0:T(8,128)} %fusion.89) | copy-start | bytes 1327108
  320.2 25.2 %copy-start.17 = (f32[12,144,144]{1,2,0:T(8,128)S(1)}, f32[12,144,144]{1,2,0:T(8,128)}, u32[]{:S(2)}) copy-start(f32[12,144,144]{1,2,0:T(8,128)} %copy-done.15) | copy-start | bytes 2985988
  320.2 16.7 %collective-permute-start.17 = (bf16[1,144,12,64]{1,3,2,0:T(8,128)(2,1)S(1)}, bf16[1,144,12,64]{1,3,2,0:T(8,128)(2,1)S(1)}, u32[]{:S(2)}, u32[]{:S(2)}) collective-permute-start(bf16[1,144,12,64]{1,3,2,0:T(8,128)(2,1)S(1)} %add_convert_fusion.8), channel_id=1, source_target_pairs={{3,0},{0,1},{1,2},{2,3},{7,4},{4,5},{5,6},{6,7},{11,8},{8,9},{9,10... | collective-permute-start | bytes 663560 | tf_op jit(solution)/shard_map/ppermute | solution.py:16
  329.9 15.4 %collective-permute-start.21 = (bf16[1,144,12,64]{1,3,2,0:T(8,128)(2,1)S(1)}, bf16[1,144,12,64]{1,3,2,0:T(8,128)(2,1)S(1)}, u32[]{:S(2)}, u32[]{:S(2)}) collective-permute-start(bf16[1,144,12,64]{1,3,2,0:T(8,128)(2,1)S(1)} %fusion.101), channel_id=1, source_target_pairs={{3,0},{0,1},{1,2},{2,3},{7,4},{4,5},{5,6},{6,7},{11,8},{8,9},{9,10... | collective-permute-start | bytes 663560 | tf_op jit(solution)/shard_map/ppermute | solution.py:16
  337.0 15.3 %copy-start.270 = (f32[1,1,144]{2,1,0:T(1,128)S(1)}, f32[1,1,144]{2,1,0:T(1,128)}, u32[]{:S(2)}) copy-start(f32[1,1,144]{2,1,0:T(1,128)} %copy-done.268) | copy-start | bytes 1732
  337.0 15.2 %collective-permute-start.18 = (bf16[1,144,12,64]{1,3,2,0:T(8,128)(2,1)S(1)}, bf16[1,144,12,64]{1,3,2,0:T(8,128)(2,1)S(1)}, u32[]{:S(2)}, u32[]{:S(2)}) collective-permute-start(bf16[1,144,12,64]{1,3,2,0:T(8,128)(2,1)S(1)} %add_convert_fusion.7), channel_id=1, source_target_pairs={{3,0},{0,1},{1,2},{2,3},{7,4},{4,5},{5,6},{6,7},{11,8},{8,9},{9,10... | collective-permute-start | bytes 663560 | tf_op jit(solution)/shard_map/ppermute | solution.py:16
  346.8 10.3 %collective-permute-start.22 = (bf16[1,144,12,64]{1,3,2,0:T(8,128)(2,1)S(1)}, bf16[1,144,12,64]{1,3,2,0:T(8,128)(2,1)S(1)}, u32[]{:S(2)}, u32[]{:S(2)}) collective-permute-start(bf16[1,144,12,64]{1,3,2,0:T(8,128)(2,1)S(1)} %fusion.100), channel_id=1, source_target_pairs={{3,0},{0,1},{1,2},{2,3},{7,4},{4,5},{5,6},{6,7},{11,8},{8,9},{9,10... | collective-permute-start | bytes 663560 | tf_op jit(solution)/shard_map/ppermute | solution.py:16
  468.8 101.5 %collective-permute-start.23 = (bf16[1,144,12,64]{1,3,2,0:T(8,128)(2,1)}, bf16[1,144,12,64]{1,3,2,0:T(8,128)(2,1)}, u32[]{:S(2)}, u32[]{:S(2)}) collective-permute-start(bf16[1,144,12,64]{1,3,2,0:T(8,128)(2,1)} %fusion.112), channel_id=1, source_target_pairs={{3,0},{0,1},{1,2},{2,3},{7,4},{4,5},{5,6},{6,7},{11,8},{8,9},{9,10... | collective-permute-start | bytes 663560 | tf_op jit(solution)/shard_map/ppermute | solution.py:16
  474.0 98.5 %collective-permute-start.27 = (bf16[1,144,12,64]{1,3,2,0:T(8,128)(2,1)}, bf16[1,144,12,64]{1,3,2,0:T(8,128)(2,1)}, u32[]{:S(2)}, u32[]{:S(2)}) collective-permute-start(bf16[1,144,12,64]{1,3,2,0:T(8,128)(2,1)} %fusion.111), channel_id=1, source_target_pairs={{3,0},{0,1},{1,2},{2,3},{7,4},{4,5},{5,6},{6,7},{11,8},{8,9},{9,10... | collective-permute-start | bytes 663560 | tf_op jit(solution)/shard_map/ppermute | solution.py:16
  571.8 14.3 %copy-start.90 = (f32[1,144,12,64]{1,3,2,0:T(8,128)S(1)}, f32[1,144,12,64]{1,3,2,0:T(8,128)}, u32[]{:S(2)}) copy-start(f32[1,144,12,64]{1,3,2,0:T(8,128)} %fusion.85) | copy-start | bytes 1327108
  571.8 14.3 %collective-permute-start.24 = (bf16[1,144,12,64]{1,3,2,0:T(8,128)(2,1)S(1)}, bf16[1,144,12,64]{1,3,2,0:T(8,128)(2,1)S(1)}, u32[]{:S(2)}, u32[]{:S(2)}) collective-permute-start(bf16[1,144,12,64]{1,3,2,0:T(8,128)(2,1)S(1)} %add_convert_fusion.5), channel_id=1, source_target_pairs={{3,0},{0,1},{1,2},{2,3},{7,4},{4,5},{5,6},{6,7},{11,8},{8,9},{9,10... | collective-permute-start | bytes 663560 | tf_op jit(solution)/shard_map/ppermute | solution.py:16
  575.0 19.5 %collective-permute-start.28 = (bf16[1,144,12,64]{1,3,2,0:T(8,128)(2,1)S(1)}, bf16[1,144,12,64]{1,3,2,0:T(8,128)(2,1)S(1)}, u32[]{:S(2)}, u32[]{:S(2)}) collective-permute-start(bf16[1,144,12,64]{1,3,2,0:T(8,128)(2,1)S(1)} %add_convert_fusion.2), channel_id=1, source_target_pairs={{3,0},{0,1},{1,2},{2,3},{7,4},{4,5},{5,6},{6,7},{11,8},{8,9},{9,10... | collective-permute-start | bytes 663560 | tf_op jit(solution)/shard_map/ppermute | solution.py:16
  586.2 16.7 %copy-start.89 = (f32[1,144,12,64]{1,3,2,0:T(8,128)S(1)}, f32[1,144,12,64]{1,3,2,0:T(8,128)}, u32[]{:S(2)}) copy-start(f32[1,144,12,64]{1,3,2,0:T(8,128)} %fusion.84) | copy-start | bytes 1327108
  586.2 25.1 %copy-start.14 = (f32[12,144,144]{1,2,0:T(8,128)S(1)}, f32[12,144,144]{1,2,0:T(8,128)}, u32[]{:S(2)}) copy-start(f32[12,144,144]{1,2,0:T(8,128)} %copy-done.12) | copy-start | bytes 2985988
  586.2 16.7 %collective-permute-start.25 = (bf16[1,144,12,64]{1,3,2,0:T(8,128)(2,1)S(1)}, bf16[1,144,12,64]{1,3,2,0:T(8,128)(2,1)S(1)}, u32[]{:S(2)}, u32[]{:S(2)}) collective-permute-start(bf16[1,144,12,64]{1,3,2,0:T(8,128)(2,1)S(1)} %add_convert_fusion.4), channel_id=1, source_target_pairs={{3,0},{0,1},{1,2},{2,3},{7,4},{4,5},{5,6},{6,7},{11,8},{8,9},{9,10... | collective-permute-start | bytes 663560 | tf_op jit(solution)/shard_map/ppermute | solution.py:16
  595.9 15.4 %collective-permute-start.29 = (bf16[1,144,12,64]{1,3,2,0:T(8,128)(2,1)S(1)}, bf16[1,144,12,64]{1,3,2,0:T(8,128)(2,1)S(1)}, u32[]{:S(2)}, u32[]{:S(2)}) collective-permute-start(bf16[1,144,12,64]{1,3,2,0:T(8,128)(2,1)S(1)} %fusion.99), channel_id=1, source_target_pairs={{3,0},{0,1},{1,2},{2,3},{7,4},{4,5},{5,6},{6,7},{11,8},{8,9},{9,10... | collective-permute-start | bytes 663560 | tf_op jit(solution)/shard_map/ppermute | solution.py:16
  603.1 12.9 %copy-start.86 = (f32[1,144,12,64]{1,3,2,0:T(8,128)S(1)}, f32[1,144,12,64]{1,3,2,0:T(8,128)}, u32[]{:S(2)}) copy-start(f32[1,144,12,64]{1,3,2,0:T(8,128)} %copy-done.85) | copy-start | bytes 1327108
  603.1 12.9 %copy-start.88 = (f32[1,144,12,64]{1,3,2,0:T(8,128)S(1)}, f32[1,144,12,64]{1,3,2,0:T(8,128)}, u32[]{:S(2)}) copy-start(f32[1,144,12,64]{1,3,2,0:T(8,128)} %copy-done.87) | copy-start | bytes 1327108
  603.1 12.9 %copy-start.259 = (f32[12,32]{1,0:T(8,128)S(1)}, f32[12,32]{1,0:T(8,128)}, u32[]{:S(2)}) copy-start(f32[12,32]{1,0:T(8,128)} %copy-done.258) | copy-start | bytes 4612
  603.1 12.8 %collective-permute-start.26 = (bf16[1,144,12,64]{1,3,2,0:T(8,128)(2,1)S(1)}, bf16[1,144,12,64]{1,3,2,0:T(8,128)(2,1)S(1)}, u32[]{:S(2)}, u32[]{:S(2)}) collective-permute-start(bf16[1,144,12,64]{1,3,2,0:T(8,128)(2,1)S(1)} %add_convert_fusion.3), channel_id=1, source_target_pairs={{3,0},{0,1},{1,2},{2,3},{7,4},{4,5},{5,6},{6,7},{11,8},{8,9},{9,10... | collective-permute-start | bytes 663560 | tf_op jit(solution)/shard_map/ppermute | solution.py:16
  613.6 29.4 %collective-permute-start.30 = (bf16[1,144,12,64]{1,3,2,0:T(8,128)(2,1)}, bf16[1,144,12,64]{1,3,2,0:T(8,128)(2,1)}, u32[]{:S(2)}, u32[]{:S(2)}) collective-permute-start(bf16[1,144,12,64]{1,3,2,0:T(8,128)(2,1)} %fusion.98), channel_id=1, source_target_pairs={{3,0},{0,1},{1,2},{2,3},{7,4},{4,5},{5,6},{6,7},{11,8},{8,9},{9,10... | collective-permute-start | bytes 663560 | tf_op jit(solution)/shard_map/ppermute | solution.py:16
  (312 other events, 1102.5 us)
